TPU v7x, 128 devices: a whole 4x4x4 slice. The times are simulated.
128 devices in a mesh: section: 2 (over z_hi), dp: 64 (over z_lo, x, y, core).
Axes of the slice: x: 4, y: 4, z: 4 (z_hi: 2, z_lo: 2; z = z_hi * 2 + z_lo), core: 2. Of those that a mesh axis runs over, the one named last changes fastest.
Arguments:
- content_in: bfloat16 [16384, 768], P('dp'), may hold values from -6 to 6
- query_in: bfloat16 [2432, 768], P('dp'), may hold values from -6 to 6
- content_cot: bfloat16 [16384, 768], P('dp'), may hold values from -6 to 6
- query_cot: bfloat16 [2432, 768], P('dp'), may hold values from -6 to 6
- order_rank: int32 [128, 128], P('dp'), may hold values from 0 to 127, each once within a row
- query_pos: int32 [128, 19], P('dp'), may hold values from 0 to 127, as said below
- group_tag: int32 [128, 128], P('dp'), may hold values from 0 to 2, as said below
- w_query: bfloat16 [2, 768, 768], P('section'), may hold values from -0.3125 to 0.3125
- b_query: float32 [2, 768], P('section'), may hold values from -3 to 3
- w_key: bfloat16 [2, 768, 768], P('section'), may hold values from -0.21875 to 0.21875
- w_value: bfloat16 [2, 768, 768], P('section'), may hold values from -0.21875 to 0.21875
- b_value: float32 [2, 768], P('section'), may hold values from -3 to 3
- w_out: bfloat16 [2, 768, 768], P('section'), may hold values from -0.875 to 0.875
- b_out: float32 [2, 768], P('section'), may hold values from -3 to 3
- norm1_gain: float32 [2, 768], P('section'), may hold values from 0.5 to 1.5
- norm1_bias: float32 [2, 768], P('section'), may hold values from -2 to 2
- w_expand: bfloat16 [2, 768, 3072], P('section'), may hold values from -0.21875 to 0.21875
- b_expand: float32 [2, 3072], P('section'), may hold values from -3 to 3
- w_contract: bfloat16 [2, 3072, 768], P('section'), may hold values from -0.109375 to 0.109375
- b_contract: float32 [2, 768], P('section'), may hold values from -3 to 3
- norm2_gain: float32 [2, 768], P('section'), may hold values from 0.5 to 1.5
- norm2_bias: float32 [2, 768], P('section'), may hold values from -2 to 2
- rel_table: float32 [32, 12], replicated, may hold values from -6 to 6
Outputs:
- content_ends: float32 [2, 16384, 768], P('section', 'dp')
- query_ends: float32 [2, 2432, 768], P('section', 'dp')
- grad_w_query: float32 [2, 768, 768], P('section')
- grad_b_query: float32 [2, 768], P('section')
- grad_w_key: float32 [2, 768, 768], P('section')
- grad_w_value: float32 [2, 768, 768], P('section')
- grad_b_value: float32 [2, 768], P('section')
- grad_w_out: float32 [2, 768, 768], P('section')
- grad_b_out: float32 [2, 768], P('section')
- grad_norm1_gain: float32 [2, 768], P('section')
- grad_norm1_bias: float32 [2, 768], P('section')
- grad_w_expand: float32 [2, 768, 3072], P('section')
- grad_b_expand: float32 [2, 3072], P('section')
- grad_w_contract: float32 [2, 3072, 768], P('section')
- grad_b_contract: float32 [2, 768], P('section')
- grad_norm2_gain: float32 [2, 768], P('section')
- grad_norm2_bias: float32 [2, 768], P('section')
- grad_rel_table: float32 [32, 12], replicated
Inputs may be any that keep to these rules, and one draw needn't show every extreme that they name: `query_pos`: each sequence's 19 entries are distinct positions. `group_tag`: tags never fall along a sequence; each sequence holds three groups of 32 or more positions.
All inputs are finite; a program needn't handle non-finite values.
Results may differ from a plain program's by a relative error of at most 0.025.
Values may be sent and summed in bfloat16 or wider, within the bound.
No kernel may reach another device: no remote copies, remote signals or barrier semaphores. Data moves between devices by JAX's collectives and lax.ppermute only.
A program may use at most 256 MiB of HBM per device.

v0:
```python
import jax
import jax.numpy as jnp
from jax import lax
from jax.experimental import pallas as pl
from jax.experimental.pallas import tpu as pltpu
from jax.sharding import PartitionSpec as P

D = 768
H = 12
HD = 64
FF = 3072
NB = 32
L = 128
PAIRS = H // 2
SEQS = 2
CONTENT = SEQS * L
PICKS = 32
ROWS = CONTENT + SEQS * PICKS
SEQ_ROWS = L + PICKS
EPSILON = 1e-05
SCALE = HD ** (-0.5)
TILE = 512
BAND = 32
LOW = jnp.bfloat16
WIDE = jnp.float32


def nn(former, latter):
    return lax.dot_general(
        former, latter, (((1,), (0,)), ((), ())), preferred_element_type=WIDE
    )


def nt(former, latter):
    return lax.dot_general(
        former, latter, (((1,), (1,)), ((), ())), preferred_element_type=WIDE
    )


def tn(former, latter):
    return lax.dot_general(
        former, latter, (((0,), (0,)), ((), ())), preferred_element_type=WIDE
    )


def seq_rows(ref, seq, lanes):
    return jnp.concatenate(
        [
            ref[seq * L : (seq + 1) * L, lanes],
            ref[CONTENT + seq * PICKS : CONTENT + (seq + 1) * PICKS, lanes],
        ]
    )


def store_rows(ref, seq, lanes, value):
    ref[seq * L : (seq + 1) * L, lanes] = value[:L]
    ref[CONTENT + seq * PICKS : CONTENT + (seq + 1) * PICKS, lanes] = value[L:]


def halves(value):
    even = lax.broadcasted_iota(jnp.int32, value.shape, 1) < HD
    zero = jnp.zeros_like(value)
    return jnp.concatenate([jnp.where(even, value, zero), jnp.where(even, zero, value)])


def side(value):
    count = value.shape[0] // 2
    return jnp.concatenate([value[:count], value[count:]], axis=1)


def bands(body):
    def step(index, carry):
        body(pl.ds(pl.multiple_of(index * BAND, BAND), BAND))
        return carry

    lax.fori_loop(0, ROWS // BAND, step, 0)


def pairs_loop(body):
    def step(pair, carry):
        body(pair, pl.ds(pl.multiple_of(pair * 128, 128), 128))
        return carry

    lax.fori_loop(0, PAIRS, step, 0)


def tiles_loop(body):
    def step(tile, carry):
        body(pl.ds(pl.multiple_of(tile * TILE, TILE), TILE))
        return carry

    lax.fori_loop(0, FF // TILE, step, 0)


def norm_rows(values):
    centered = values - jnp.mean(values, axis=-1, keepdims=True)
    variance = jnp.mean(centered * centered, axis=-1, keepdims=True)
    root = lax.rsqrt(variance + EPSILON)
    return (centered * root, root)


def norm_rows_back(scaled, normed, root):
    return root * (
        scaled
        - jnp.mean(scaled, axis=-1, keepdims=True)
        - normed * jnp.mean(scaled * normed, axis=-1, keepdims=True)
    )


B_QUERY, B_VALUE, B_OUT, GAIN1, SHIFT1, B_CONTRACT, GAIN2, SHIFT2 = range(8)


def forward(x, w, vec, b_expand, masks, s, keep, ready):
    row = lambda k: vec[k : k + 1, :]
    ready("query")
    s.query[...] = (nn(x[...], w.query[...]) + row(B_QUERY)).astype(LOW)
    ready("key")
    s.key[...] = nn(x[:CONTENT], w.key[...]).astype(LOW)
    ready("value")
    s.value[...] = (nn(x[:CONTENT], w.value[...]) + row(B_VALUE)).astype(LOW)
    ready("masks")

    def attend(pair, lanes):
        for seq in range(SEQS):
            own = pl.ds(seq * L, L)
            scores = (
                nt(halves(seq_rows(s.query, seq, lanes)), s.key[own, lanes]) * SCALE
                + masks[seq, pair]
            )
            shifted = jnp.exp(scores - jnp.max(scores, axis=-1, keepdims=True))
            probs = (shifted / jnp.sum(shifted, axis=-1, keepdims=True)).astype(LOW)
            if keep:
                s.probs[seq, pair] = probs
            mixed = nn(side(probs), halves(s.value[own, lanes]))
            store_rows(s.mixed, seq, lanes, mixed.astype(LOW))

    pairs_loop(attend)
    ready("out")
    s.total[...] = nn(s.mixed[...], w.out[...])

    def first_norm(band):
        normed, root = norm_rows(x[band].astype(WIDE) + s.total[band] + row(B_OUT))
        first = normed * row(GAIN1) + row(SHIFT1)
        s.first_low[band] = first.astype(LOW)
        s.total[band] = first + row(B_CONTRACT)
        if keep:
            s.normed1[band] = normed
            s.root1[band] = jnp.broadcast_to(root, (BAND, 128))

    bands(first_norm)
    ready("expand")
    ready("contract")

    def feed(tile):
        expanded = nn(s.first_low[...], w.expand[:, tile]) + b_expand[:, tile]
        cumulative = 0.5 * (1.0 + lax.erf(expanded * 0.7071067811865476))
        activated = (expanded * cumulative).astype(LOW)
        if keep:
            s.slope[:, tile] = (
                cumulative + expanded * jnp.exp(-0.5 * expanded * expanded) * 0.3989422804014327
            ).astype(LOW)
            s.activated[:, tile] = activated
        s.total[...] += nn(activated, w.contract[tile, :])

    tiles_loop(feed)

    def second_norm(band):
        normed, root = norm_rows(s.total[band])
        if keep:
            s.normed2[band] = normed
            s.root2[band] = jnp.broadcast_to(root, (BAND, 128))
        s.out[band] = (normed * row(GAIN2) + row(SHIFT2)).astype(s.out.dtype)

    bands(second_norm)


def backward_feed(grad, w, vec, s, sums=None):
    row = lambda k: vec[k : k + 1, :]

    def second_norm(band):
        upper = grad[band].astype(WIDE)
        normed = s.normed2[band]
        lower = norm_rows_back(upper * row(GAIN2), normed, s.root2[band, :1])
        s.total[band] = lower
        s.branch[band] = lower.astype(LOW)
        if sums is not None:
            sums(band, 10, upper * normed)
            sums(band, 11, upper)
            sums(band, 9, lower.astype(LOW).astype(WIDE))

    bands(second_norm)


def backward_expand(w, vec, s, sums=None, tile_sums=None):
    row = lambda k: vec[k : k + 1, :]

    def feed(tile):
        lower = (nt(s.branch[...], w.contract[tile, :]) * s.slope[:, tile].astype(WIDE)).astype(LOW)
        s.expanded[:, tile] = lower
        if tile_sums is not None:
            tile_sums(tile, lower)
        s.total[...] += nt(lower, w.expand[:, tile])

    tiles_loop(feed)

    def first_norm(band):
        upper = s.total[band]
        normed = s.normed1[band]
        lower = norm_rows_back(upper * row(GAIN1), normed, s.root1[band, :1])
        s.total[band] = lower
        s.attended[band] = lower.astype(LOW)
        if sums is not None:
            sums(band, 3, upper * normed)
            sums(band, 4, upper)
            sums(band, 2, lower.astype(LOW).astype(WIDE))

    bands(first_norm)


def backward_attend(w, s, table=None):
    s.dmixed[...] = nt(s.attended[...], w.out[...]).astype(LOW)

    def attend(pair, lanes):
        slopes = []
        for seq in range(SEQS):
            own = pl.ds(seq * L, L)
            probs = s.probs[seq, pair]
            below = halves(seq_rows(s.dmixed, seq, lanes))
            dprobs = nt(below, s.value[own, lanes])
            s.dvalue[own, lanes] = tn(probs, below).astype(LOW)
            weight = probs.astype(WIDE)
            dscores = (
                weight * (dprobs - jnp.sum(weight * dprobs, axis=-1, keepdims=True))
            ).astype(LOW)
            dquery = nn(side(dscores), halves(s.key[own, lanes])) * SCALE
            store_rows(s.dquery, seq, lanes, dquery.astype(LOW))
            dkey = tn(dscores, halves(seq_rows(s.query, seq, lanes))) * SCALE
            s.dkey[own, lanes] = dkey.astype(LOW)
            slopes.append(dscores)
        if table is not None:
            table(pair, slopes)

    pairs_loop(attend)
    s.total[...] += nt(s.dquery[...], w.query[...])
    s.total[:CONTENT] += nt(s.dkey[...], w.key[...]) + nt(s.dvalue[...], w.value[...])


class Names:
    def __init__(self, **named):
        self.__dict__.update(named)


MATRICES = ("query", "key", "value", "out", "expand", "contract")
MATRIX_SHAPES = {
    "query": (D, D),
    "key": (D, D),
    "value": (D, D),
    "out": (D, D),
    "expand": (D, FF),
    "contract": (FF, D),
}
MASK_SHAPE = (SEQS, PAIRS, 2 * SEQ_ROWS, L)
KEPT = {
    "query": ((ROWS, D), LOW),
    "key": ((CONTENT, D), LOW),
    "value": ((CONTENT, D), LOW),
    "probs": (MASK_SHAPE, LOW),
    "mixed": ((ROWS, D), LOW),
    "normed1": ((ROWS, D), WIDE),
    "root1": ((ROWS, 128), WIDE),
    "first_low": ((ROWS, D), LOW),
    "slope": ((ROWS, FF), LOW),
    "activated": ((ROWS, FF), LOW),
    "normed2": ((ROWS, D), WIDE),
    "root2": ((ROWS, 128), WIDE),
}
PASSED = {
    "branch": ((ROWS, D), LOW),
    "expanded": ((ROWS, FF), LOW),
    "attended": ((ROWS, D), LOW),
    "dmixed": ((ROWS, D), LOW),
    "dvalue": ((CONTENT, D), LOW),
    "dquery": ((ROWS, D), LOW),
    "dkey": ((CONTENT, D), LOW),
}
ANY = pl.BlockSpec(memory_space=pl.ANY)
VMEM = pl.BlockSpec(memory_space=pltpu.VMEM)
LIMIT = 60 * 1024 * 1024


def fetcher(pairs, sems):
    copies = {}
    for index, (name, source, target) in enumerate(pairs):
        copies[name] = pltpu.make_async_copy(source, target, sems.at[index])
        copies[name].start()
    return lambda name: copies[name].wait()


def front_kernel(x, *refs):
    matrices, (masks, vec, b_expand, out), rest = refs[:6], refs[6:10], refs[10:]
    held, (mask_buf, query, key, value, mixed, first_low, total, sems) = rest[:6], rest[6:]
    ready = fetcher(
        [(n, a, b) for n, a, b in zip(MATRICES[:3], matrices[:3], held[:3])]
        + [("masks", masks, mask_buf)]
        + [(n, a, b) for n, a, b in zip(MATRICES[3:], matrices[3:], held[3:])],
        sems,
    )
    s = Names(
        query=query, key=key, value=value, mixed=mixed, first_low=first_low, total=total, out=out
    )
    forward(x, Names(**dict(zip(MATRICES, held))), vec, b_expand, mask_buf, s, False, ready)


def front(x, matrices, masks, vec, b_expand):
    return pl.pallas_call(
        front_kernel,
        out_shape=jax.ShapeDtypeStruct((ROWS, D), LOW),
        in_specs=[VMEM] + [ANY] * 7 + [VMEM] * 2,
        out_specs=VMEM,
        scratch_shapes=[pltpu.VMEM(MATRIX_SHAPES[n], LOW) for n in MATRICES]
        + [pltpu.VMEM(MASK_SHAPE, WIDE)]
        + [pltpu.VMEM(*KEPT[n]) for n in ("query", "key", "value", "mixed", "first_low")]
        + [pltpu.VMEM((ROWS, D), WIDE), pltpu.SemaphoreType.DMA((7,))],
        compiler_params=pltpu.CompilerParams(vmem_limit_bytes=LIMIT),
        name="front",
    )(x, *matrices, masks, vec, b_expand)


def middle_kernel(x, cot, *refs):
    matrices, (masks, vec, b_expand), rest = refs[:6], refs[6:9], refs[9:]
    (out, grad), rest = rest[:2], rest[2:]
    kept_out, rest = rest[: len(KEPT)], rest[len(KEPT) :]
    held, (mask_buf,), rest = rest[:6], rest[6:7], rest[7:]
    kept, rest = rest[: len(KEPT)], rest[len(KEPT) :]
    passed, rest = rest[: len(PASSED)], rest[len(PASSED) :]
    total, sems, out_sems = rest
    ready = fetcher(
        [(n, a, b) for n, a, b in zip(MATRICES[:3], matrices[:3], held[:3])]
        + [("masks", masks, mask_buf)]
        + [(n, a, b) for n, a, b in zip(MATRICES[3:], matrices[3:], held[3:])],
        sems,
    )
    w = Names(**dict(zip(MATRICES, held)))
    s = Names(total=total, out=out, **dict(zip(KEPT, kept)), **dict(zip(PASSED, passed)))
    forward(x, w, vec, b_expand, mask_buf, s, True, ready)
    done = fetcher([(n, a, b) for n, a, b in zip(KEPT, kept, kept_out)], out_sems)
    backward_feed(cot, w, vec, s)
    backward_expand(w, vec, s)
    backward_attend(w, s)
    grad[...] = total[...].astype(LOW)
    for name in KEPT:
        done(name)


def middle(x, cot, matrices, masks, vec, b_expand):
    return pl.pallas_call(
        middle_kernel,
        out_shape=[
            jax.ShapeDtypeStruct((ROWS, D), WIDE),
            jax.ShapeDtypeStruct((ROWS, D), LOW),
        ]
        + [jax.ShapeDtypeStruct(*KEPT[n]) for n in KEPT],
        in_specs=[VMEM] * 2 + [ANY] * 7 + [VMEM] * 2,
        out_specs=[VMEM] * 2 + [ANY] * len(KEPT),
        scratch_shapes=[pltpu.VMEM(MATRIX_SHAPES[n], LOW) for n in MATRICES]
        + [pltpu.VMEM(MASK_SHAPE, WIDE)]
        + [pltpu.VMEM(*KEPT[n]) for n in KEPT]
        + [pltpu.VMEM(*PASSED[n]) for n in PASSED]
        + [
            pltpu.VMEM((ROWS, D), WIDE),
            pltpu.SemaphoreType.DMA((7,)),
            pltpu.SemaphoreType.DMA((len(KEPT),)),
        ],
        compiler_params=pltpu.CompilerParams(vmem_limit_bytes=LIMIT),
        name="middle",
    )(x, cot, *matrices, masks, vec, b_expand)


QUARTER = D // 4
BLOCKS = 6


def back_kernel(x, upper, spread, *refs):
    matrices, (vec,), rest = refs[:6], refs[6:7], refs[7:]
    kept_in, rest = rest[: len(KEPT)], rest[len(KEPT) :]
    (grad, small, table, groups), rest = rest[:4], rest[4:]
    held, rest = rest[:6], rest[6:]
    kept, rest = rest[: len(KEPT)], rest[len(KEPT) :]
    passed, rest = rest[: len(PASSED)], rest[len(PASSED) :]
    total, stage, sems, out_sems = rest
    first = ("normed2", "root2", "activated")
    later = [n for n in KEPT if n not in first]
    kept_pairs = {n: (n, a, b) for n, a, b in zip(KEPT, kept_in, kept)}
    matrix_pairs = {n: ("w_" + n, a, b) for n, a, b in zip(MATRICES, matrices, held)}
    ready = fetcher(
        [kept_pairs[n] for n in first]
        + [matrix_pairs["contract"], kept_pairs["slope"], matrix_pairs["expand"]]
        + [kept_pairs[n] for n in later if n != "slope"]
        + [matrix_pairs[n] for n in ("out", "query", "key", "value")],
        sems,
    )
    w = Names(**dict(zip(MATRICES, held)))
    s = Names(total=total, **dict(zip(KEPT, kept)), **dict(zip(PASSED, passed)))
    small[...] = jnp.zeros_like(small)

    def sums(band, place, value):
        small[place : place + 1, :] += jnp.sum(value, axis=0, keepdims=True)

    for name in first:
        ready(name)
    backward_feed(upper, w, vec, s, sums)

    pending = []

    def emit(core, quarter, block, value):
        slot = len(pending) % 2
        if len(pending) >= 2:
            pending[-2].wait()
        stage[slot] = value.astype(LOW)
        copy = pltpu.make_async_copy(
            stage.at[slot], groups.at[core, quarter, block], out_sems.at[slot]
        )
        copy.start()
        pending.append(copy)

    for index in range(FF // QUARTER):
        core, block, quarter = index // 8, index // 4 % 2, index % 4
        emit(
            core,
            quarter,
            block,
            tn(s.activated[:, index * QUARTER : (index + 1) * QUARTER], s.branch[...]),
        )

    def tile_sums(tile, value):
        pass

    ready("w_contract")
    ready("slope")
    ready("w_expand")
    for name in later:
        if name != "slope":
            ready(name)
    backward_expand(w, vec, s, sums, tile_sums)
    for column in range(4):
        part = jnp.sum(s.expanded[:, column * D : (column + 1) * D].astype(WIDE), axis=0, keepdims=True)
        small[5 + column : 6 + column, :] = part
        for quarter in range(4):
            emit(
                column // 2,
                quarter,
                2 + column % 2,
                tn(
                    s.first_low[:, quarter * QUARTER : (quarter + 1) * QUARTER],
                    s.expanded[:, column * D : (column + 1) * D],
                ),
            )
    for name in ("out", "query", "key", "value"):
        ready("w_" + name)

    def table_sum(pair, slopes):
        both = jnp.concatenate([slope[:SEQ_ROWS] for slope in slopes])
        table[2 * pair] = nn(spread[...], both)
        both = jnp.concatenate([slope[SEQ_ROWS:] for slope in slopes])
        table[2 * pair + 1] = nn(spread[...], both)

    backward_attend(w, s, table_sum)
    grad[...] = total[...]
    small[0:1, :] = jnp.sum(s.dquery[...].astype(WIDE), axis=0, keepdims=True)
    small[1:2, :] = jnp.sum(s.dvalue[...].astype(WIDE), axis=0, keepdims=True)
    for number, (former, latter) in enumerate(
        ((x, s.dquery), (x, s.dkey), (x, s.dvalue), (s.mixed, s.attended))
    ):
        count = latter.shape[0]
        for quarter in range(4):
            emit(
                number // 2,
                quarter,
                4 + number % 2,
                tn(former[:count, quarter * QUARTER : (quarter + 1) * QUARTER], latter[...]),
            )
    pending[-2].wait()
    pending[-1].wait()


def back(x, upper, spread, matrices, vec, kept):
    copies = len(KEPT) + len(MATRICES)
    return pl.pallas_call(
        back_kernel,
        out_shape=[
            jax.ShapeDtypeStruct((ROWS, D), WIDE),
            jax.ShapeDtypeStruct((16, D), WIDE),
            jax.ShapeDtypeStruct((H, L, L), WIDE),
            jax.ShapeDtypeStruct((2, 4, BLOCKS, QUARTER, D), LOW),
        ],
        in_specs=[VMEM] * 3 + [ANY] * 6 + [VMEM] + [ANY] * len(KEPT),
        out_specs=[VMEM] * 3 + [ANY],
        scratch_shapes=[pltpu.VMEM(MATRIX_SHAPES[n], LOW) for n in MATRICES]
        + [pltpu.VMEM(*KEPT[n]) for n in KEPT]
        + [pltpu.VMEM(*PASSED[n]) for n in PASSED]
        + [
            pltpu.VMEM((ROWS, D), WIDE),
            pltpu.VMEM((2, QUARTER, D), LOW),
            pltpu.SemaphoreType.DMA((copies,)),
            pltpu.SemaphoreType.DMA((2,)),
        ],
        compiler_params=pltpu.CompilerParams(vmem_limit_bytes=LIMIT),
        name="back",
    )(x, upper, spread, *matrices, vec, *kept)


LIMITS = (12, 16, 23, 32, 46, 64, 91)
TOP_PRECISION = lax.Precision.HIGHEST


def bucket_of(relative):
    distance = jnp.abs(relative)
    beyond = 8 + sum(((distance >= limit).astype(jnp.int32) for limit in LIMITS))
    within = jnp.where(distance < 8, distance, beyond)
    return within + 16 * (relative > 0).astype(jnp.int32)


def geometry(order_row, pos_row, tag_row, table):
    positions = lax.iota(jnp.int32, L)
    matches = pos_row[:, None] == positions[None, :]
    predicted = jnp.any(matches, axis=0)
    query_rank = jnp.sum(jnp.where(matches, order_row[None, :], 0), axis=1)
    query_tag = jnp.sum(jnp.where(matches, tag_row[None, :], 0), axis=1)
    row_rank = jnp.concatenate([order_row, query_rank])
    row_tag = jnp.concatenate([tag_row, query_tag])
    row_place = jnp.concatenate([positions, pos_row])
    row_flag = jnp.concatenate([predicted, jnp.ones(pos_row.shape, jnp.bool_)])
    strict = jnp.concatenate([jnp.zeros((L,), jnp.int32), jnp.ones(pos_row.shape, jnp.int32)])
    same_group = row_tag[:, None] == tag_row[None, :]
    earlier = order_row[None, :] + strict[:, None] <= row_rank[:, None]
    allowed = same_group & (~predicted[None, :] | row_flag[:, None] & earlier)
    buckets = bucket_of(positions[None, :] - row_place[:, None])
    one_hot = (buckets[None] == lax.iota(jnp.int32, NB)[:, None, None]).astype(WIDE)
    score_bias = jnp.einsum("krl,kh->hrl", one_hot, table, precision=TOP_PRECISION)
    masked = jnp.where(allowed[None], score_bias, -1e30)
    masked = jnp.pad(masked, ((0, 0), (0, SEQ_ROWS - masked.shape[1]), (0, 0)))
    padded = jnp.pad(matches.astype(LOW), ((0, PICKS - matches.shape[0]), (0, 0)))
    spread = jnp.concatenate([jnp.eye(L, dtype=LOW), padded.T], axis=1)
    return (masked, spread)


def diagonals():
    positions = lax.iota(jnp.int32, L)
    buckets = bucket_of(positions[None, :] - positions[:, None])
    return (buckets[None] == lax.iota(jnp.int32, NB)[:, None, None]).astype(WIDE)


PLANE = ("x", "y", "c")


def shift(value, axis, by):
    size = lax.axis_size(axis)
    return lax.ppermute(value, axis, [(i, (i + by) % size) for i in range(size)])


def turn(value, outer, by):
    pairs = []
    for i in range(4):
        for j in range(4):
            for c in range(2):
                if (c == 0) == outer:
                    target = ((i + by) % 4, j)
                else:
                    target = (i, (j + by) % 4)
                pairs.append(((i * 4 + j) * 2 + c, (target[0] * 4 + target[1]) * 2 + c))
    return lax.ppermute(value, PLANE, pairs)


def place(outer):
    return jnp.where(
        (lax.axis_index("c") == 0) == outer, lax.axis_index("x"), lax.axis_index("y")
    )


def wide(value):
    return value.astype(WIDE)


def pick(parts, index):
    return lax.dynamic_index_in_dim(parts, index, 0, keepdims=False)


def ring_reduce(parts, outer):
    me = place(outer)
    own, after, across, before = (pick(parts, (me + k) % 4) for k in range(4))
    half = parts.shape[1] // 2
    from_left = turn(across[:half], outer, 1)
    from_right = turn(across[half:], outer, -1)
    to_right = jnp.concatenate(
        [(wide(after[:half]) + wide(from_left)).astype(LOW), after[half:]]
    )
    to_left = jnp.concatenate(
        [before[:half], (wide(before[half:]) + wide(from_right)).astype(LOW)]
    )
    left_sum = turn(to_right, outer, 1)
    right_sum = turn(to_left, outer, -1)
    return (wide(own) + wide(left_sum) + wide(right_sum)).astype(LOW)


def direct_reduce(parts, outer):
    me = place(outer)
    total = wide(pick(parts, me))
    for by in (1, 2, -1):
        total += wide(turn(pick(parts, (me + by) % 4), outer, by))
    return total.astype(LOW)


def join(parts, outer):
    me = place(outer)
    whole = jnp.zeros((4,) + parts[0].shape, parts[0].dtype)
    for k, part in enumerate(parts):
        whole = lax.dynamic_update_index_in_dim(whole, part, (me + k) % 4, 0)
    return whole


def ring_gather(own, outer):
    half = own.shape[0] // 2
    before = turn(own, outer, 1)
    after = turn(own, outer, -1)
    across = jnp.concatenate([turn(before[:half], outer, 1), turn(after[half:], outer, -1)])
    return join((own, after, across, before), outer)


def direct_gather(own, outer):
    after, across, before = (turn(own, outer, by) for by in (-1, 2, 1))
    return join((own, after, across, before), outer)


def pair_reduce(parts, axis):
    me = lax.axis_index(axis)
    arrived = shift(pick(parts, 1 - me), axis, 1)
    return (wide(pick(parts, me)) + wide(arrived)).astype(LOW)


def pair_gather(own, axis):
    me = lax.axis_index(axis)
    arrived = shift(own, axis, 1)
    return jnp.where(me == 0, jnp.stack([own, arrived]), jnp.stack([arrived, own]))


def reduce_groups(groups):
    count = BLOCKS * QUARTER
    part = pair_reduce(groups.reshape(2, 4, count, D), "c")
    part = ring_reduce(part, True)
    part = direct_reduce(part.reshape(4, count // 4, D), False)
    part = pair_reduce(part.reshape(2, count // 8, D), "z")
    part = pair_gather(part, "z").reshape(count // 4, D)
    part = direct_gather(part, False).reshape(count, D)
    part = ring_gather(part, True)
    return pair_gather(part, "c").reshape(2, 4, BLOCKS, QUARTER, D)


def on_device(
    content_in,
    query_in,
    content_cot,
    query_cot,
    order_rank,
    query_pos,
    group_tag,
    *rest,
):
    (
        w_query,
        b_query,
        w_key,
        w_value,
        b_value,
        w_out,
        b_out,
        norm1_gain,
        norm1_bias,
        w_expand,
        b_expand,
        w_contract,
        b_contract,
        norm2_gain,
        norm2_bias,
    ) = (argument[0] for argument in rest[:-1])
    rel_table = rest[-1]
    is_first = lax.axis_index("s") == 0
    picks = query_pos.shape[1]

    def rows_of(content, query):
        query = jnp.pad(query.reshape(SEQS, picks, D), ((0, 0), (0, PICKS - picks), (0, 0)))
        return jnp.concatenate([content, query.reshape(SEQS * PICKS, D)])

    masks, spread = jax.vmap(geometry, in_axes=(0, 0, 0, None))(
        order_rank, query_pos, group_tag, rel_table
    )
    masks = masks.reshape(MASK_SHAPE)
    spread = jnp.concatenate([spread[0], spread[1]], axis=1)
    own_rows = rows_of(content_in, query_in)
    cotangent = rows_of(content_cot, query_cot)
    matrices = (w_query, w_key, w_value, w_out, w_expand, w_contract)
    vec = jnp.stack(
        [b_query, b_value, b_out, norm1_gain, norm1_bias, b_contract, norm2_gain, norm2_bias]
    )
    b_expand = b_expand[None]
    first_out = front(own_rows, matrices, masks, vec, b_expand)
    rows = jnp.where(is_first, own_rows, shift(first_out, "s", 1))
    output, rows_grad, *kept = middle(rows, cotangent, matrices, masks, vec, b_expand)
    upper = jnp.where(is_first, shift(rows_grad, "s", 1), cotangent)
    rows_grad, small, slopes, groups = back(rows, upper, spread, matrices, vec, kept)
    ends = jnp.where(is_first, rows_grad, output)
    content_ends = ends[None, :CONTENT]
    query_ends = ends[CONTENT:].reshape(SEQS, PICKS, D)[:, :picks].reshape(1, SEQS * picks, D)
    table = jnp.einsum("krl,hrl->kh", diagonals(), slopes, precision=TOP_PRECISION)
    table = jnp.pad(table.reshape(1, NB * H), ((0, 0), (0, D - NB * H)))
    small = jnp.concatenate([small[:12], table])
    small_sum = jnp.sum(lax.all_gather(small, DP, axis=0), axis=0)
    table_row = small_sum[12]
    table_total = (table_row + shift(table_row, "s", 1))[: NB * H].reshape(NB, H)
    groups = wide(reduce_groups(groups))
    contract = groups[:, :, 0:2].transpose(0, 2, 1, 3, 4).reshape(1, FF, D)
    expand = groups[:, :, 2:4].transpose(1, 3, 0, 2, 4).reshape(1, D, FF)
    heads = groups[:, :, 4:6].transpose(0, 2, 1, 3, 4).reshape(4, 1, D, D)
    row = lambda k: small_sum[k][None]
    return (
        content_ends,
        query_ends,
        heads[0],
        row(0),
        heads[1],
        heads[2],
        row(1),
        heads[3],
        row(2),
        row(3),
        row(4),
        expand,
        small_sum[5:9].reshape(1, FF),
        contract,
        row(9),
        row(10),
        row(11),
        table_total,
    )


DP = ("z", "x", "y", "c")


def solution(mesh):
    mesh = jax.sharding.Mesh(mesh.devices.reshape(2, 2, 4, 4, 2), ("s",) + DP)
    layer_specs = tuple(
        P("s", *([None] * (rank - 1))) for rank in (3, 2, 3, 3, 2, 3, 2, 2, 2, 3, 2, 3, 2, 2, 2)
    )
    in_specs = (P(DP, None),) * 7 + layer_specs + (P(),)
    out_specs = (P("s", DP, None),) * 2 + layer_specs + (P(),)
    return jax.shard_map(
        on_device, mesh=mesh, in_specs=in_specs, out_specs=out_specs, check_vma=False
    )
```

profile of v0, /device:TPU:0, one launch (start us, length us, event | category | flops | bytes accessed | tf_op | source)
XLA Modules:
  0.0 518.8 jit_solution(8595920921946567903)
XLA Ops:
  12.3 1.7 select_bitcast_fusion
  17.7 19.6 %front.1 = bf16[320,768]{1,0:T(8,128)(2,1)} custom-call(bf16[320,768]{1,0:T(8,128)(2,1)} %pad_maximum_fusion.2.x, bf16[768,768]{1,0:T(8,128)(2,1)} %bitcast.131, bf16[768,768]{1,0:T(8,128)(2,1)} %bitcast.134, bf16[768,768]{1,0:T(8,128)(2,1)} %bitcast.137, bf16[768,768]{1,0:T(8,128)(2,1)} %bitcast.140, bf16[768,3072]{1,0:T(8,128)(2,1)} %bitcast.120, ...), custom_call_target="tpu_custom_call" | custom-call | tf_op jit(solution)/shard_map/front/pallas_call | solution.py:315
  37.3 4.2 collective-permute-start
  42.4 10.6 %collective-permute-done = bf16[320,768]{1,0:T(8,128)(2,1)S(1)} collective-permute-done((bf16[320,768]{1,0:T(8,128)(2,1)}, bf16[320,768]{1,0:T(8,128)(2,1)S(1)}, u32[]{:S(2)}, u32[]{:S(2)}) %collective-permute-start) | collective-permute-done | bytes 491552 | tf_op jit(solution)/shard_map/ppermute | solution.py:558
  53.9 34.5 %middle.1 = (f32[320,768]{1,0:T(8,128)}, bf16[320,768]{1,0:T(8,128)(2,1)}, bf16[320,768]{1,0:T(8,128)(2,1)}, bf16[256,768]{1,0:T(8,128)(2,1)}, bf16[256,768]{1,0...) custom-call(bf16[320,768]{1,0:T(8,128)(2,1)} %broadcast_select_fusio, ...), custom_call_target="tpu_custom_call" | custom-call | tf_op jit(solution)/shard_map/middle/pallas_call | solution.py:356
  88.4 3.6 collective-permute-start.1
  92.8 10.1 %collective-permute-done.1 = bf16[320,768]{1,0:T(8,128)(2,1)S(1)} collective-permute-done((bf16[320,768]{1,0:T(8,128)(2,1)}, bf16[320,768]{1,0:T(8,128)(2,1)S(1)}, u32[]{:S(2)}, u32[]{:S(2)}) %collective-permute-start.1) | collective-permute-done | bytes 491552 | tf_op jit(solution)/shard_map/ppermute | solution.py:558
  103.8 46.4 %back.1 = (f32[320,768]{1,0:T(8,128)}, f32[16,768]{1,0:T(8,128)}, f32[12,128,128]{2,1,0:T(8,128)}, bf16[2,4,6,192,768]{4,3,2,1,0:T(8,128)(2,1)}) custom-call(bf16[320,768]{1,0:T(8,128)(2,1)} %broadcast_select_fusion.2.x, bf16[320,768]{1,0:T(8,128)(2,1)} %broadcast_select_fusion.1.upper, bf16[128,320]{1,0:T(8,128)(2,1)} %pad_maximum_fusion.4.spread, ...), custom_call_target="tpu_custom_call" | custom-call | tf_op jit(solution)/shard_map/back/pallas_call | solution.py:488
  150.2 6.4 %dynamic-slice_bitcast_fusion = bf16[4,1152,768]{2,1,0:T(8,128)(2,1)} fusion(bf16[2,4,1152,768]{3,2,1,0:T(8,128)(2,1)} %bitcast.129, s32[]{:T(128)S(6)} %select_n.204), kind=kLoop, calls=%fused_computation.7 | loop fusion | bytes 14155780 | tf_op jit(solution)/shard_map/jit(dynamic_index_in_dim)/squeeze | solution.py:585
  156.6 11.6 %collective-permute-done.2 = bf16[4,1152,768]{2,1,0:T(8,128)(2,1)} collective-permute-done((bf16[4,1152,768]{2,1,0:T(8,128)(2,1)}, bf16[4,1152,768]{2,1,0:T(8,128)(2,1)}, u32[]{:S(2)}, u32[]{:S(2)}) %collective-permute-start.2) | collective-permute-done | bytes 7077920 | tf_op jit(solution)/shard_map/ppermute | solution.py:558
  168.3 9.6 %fusion.1 = bf16[4,1152,768]{2,1,0:T(8,128)(2,1)} fusion(bf16[4,1152,768]{2,1,0:T(8,128)(2,1)} %collective-permute-done.2, bf16[2,4,1152,768]{3,2,1,0:T(8,128)(2,1)} %bitcast.130, s32[]{:T(128)S(6)} %select_n.203), kind=kLoop, calls=%fused_computation.3 | loop fusion | flops 14155776 | bytes 21233668 | tf_op jit(solution)/shard_map/convert_element_type | solution.py:637
  177.9 2.2 dynamic-slice_bitcast_fusion.5
  180.1 1.5 collective-permute-start.3
  181.6 1.8 collective-permute-start.5
  183.4 11.0 %collective-permute-done.3 = bf16[576,768]{1,0:T(8,128)(2,1)S(1)} collective-permute-done((bf16[576,768]{1,0:T(8,128)(2,1)S(1)}, bf16[576,768]{1,0:T(8,128)(2,1)S(1)}, u32[]{:S(2)}, u32[]{:S(2)}) %collective-permute-start.3) | collective-permute-done | bytes 884768 | tf_op jit(solution)/shard_map/ppermute | solution.py:571
  194.7 1.8 fusion.9
  196.7 3.0 collective-permute-start.6
  201.0 18.7 %collective-permute-done.6 = bf16[1152,768]{1,0:T(8,128)(2,1)S(1)} collective-permute-done((bf16[1152,768]{1,0:T(8,128)(2,1)S(1)}, bf16[1152,768]{1,0:T(8,128)(2,1)S(1)}, u32[]{:S(2)}, u32[]{:S(2)}) %collective-permute-start.6) | collective-permute-done | bytes 1769504 | tf_op jit(solution)/shard_map/ppermute | solution.py:571
  219.7 5.3 %collective-permute-done.4 = bf16[1152,768]{1,0:T(8,128)(2,1)} collective-permute-done((bf16[1152,768]{1,0:T(8,128)(2,1)}, bf16[1152,768]{1,0:T(8,128)(2,1)}, u32[]{:S(2)}, u32[]{:S(2)}) %collective-permute-start.4) | collective-permute-done | bytes 1769504 | tf_op jit(solution)/shard_map/ppermute | solution.py:571
  225.1 2.8 fusion.4
  228.8 1.6 collective-permute-start.7
  230.4 1.7 collective-permute-start.9
  232.1 2.0 collective-permute-start.8
  234.1 4.5 collective-permute-done.7
  238.9 5.6 %collective-permute-done.8 = bf16[288,768]{1,0:T(8,128)(2,1)S(1)} collective-permute-done((bf16[288,768]{1,0:T(8,128)(2,1)S(1)}, bf16[288,768]{1,0:T(8,128)(2,1)S(1)}, u32[]{:S(2)}, u32[]{:S(2)}) %collective-permute-start.8) | collective-permute-done | bytes 442400 | tf_op jit(solution)/shard_map/ppermute | solution.py:571
  246.0 6.8 %collective-permute-done.10 = bf16[144,768]{1,0:T(8,128)(2,1)S(1)} collective-permute-done((bf16[144,768]{1,0:T(8,128)(2,1)S(1)}, bf16[144,768]{1,0:T(8,128)(2,1)S(1)}, u32[]{:S(2)}, u32[]{:S(2)}) %collective-permute-start.10) | collective-permute-done | bytes 221216 | tf_op jit(solution)/shard_map/ppermute | solution.py:558
  254.0 4.9 collective-permute-done.11
  260.0 1.6 collective-permute-start.13
  261.7 5.6 %collective-permute-done.12 = bf16[288,768]{1,0:T(8,128)(2,1)S(1)} collective-permute-done((bf16[288,768]{1,0:T(8,128)(2,1)S(1)}, bf16[288,768]{1,0:T(8,128)(2,1)S(1)}, u32[]{:S(2)}, u32[]{:S(2)}) %collective-permute-start.12) | collective-permute-done | bytes 442400 | tf_op jit(solution)/shard_map/ppermute | solution.py:571
  267.4 2.5 collective-permute-done.13
  269.9 7.0 %collective-permute-done.14 = bf16[288,768]{1,0:T(8,128)(2,1)S(1)} collective-permute-done((bf16[288,768]{1,0:T(8,128)(2,1)S(1)}, bf16[288,768]{1,0:T(8,128)(2,1)S(1)}, u32[]{:S(2)}, u32[]{:S(2)}) %collective-permute-start.14) | collective-permute-done | bytes 442400 | tf_op jit(solution)/shard_map/ppermute | solution.py:571
  277.3 3.0 collective-permute-start.15
  280.3 20.5 %collective-permute-done.16 = bf16[1152,768]{1,0:T(8,128)(2,1)S(1)} collective-permute-done((bf16[1152,768]{1,0:T(8,128)(2,1)S(1)}, bf16[1152,768]{1,0:T(8,128)(2,1)S(1)}, u32[]{:S(2)}, u32[]{:S(2)}) %collective-permute-start.16) | collective-permute-done | bytes 1769504 | tf_op jit(solution)/shard_map/ppermute | solution.py:571
  301.0 3.3 collective-permute-start.18
  304.3 3.4 broadcast_in_dim.97
  310.3 4.8 collective-permute-done.17
  317.9 1.6 copy.60
  323.4 105.7 %all-gather.4.cloned.1.call-done = f32[64,13,768]{2,1,0:T(8,128)} async-done(((f32[1,13,768]{2,1,0:T(8,128)}), f32[64,13,768]{2,1,0:T(8,128)}) %all-gather.4.cloned.1.call-update) | async-done | bytes 2555920 | tf_op jit(solution)/shard_map/all_gather | solution.py:716
  429.1 2.1 reduce_sum.29
  431.8 3.0 collective-permute-start.20
  435.5 1.7 collective-permute-done.20
  437.9 22.1 %fusion = f32[2,4,6,192,768]{4,3,2,1,0:T(8,128)} fusion(bf16[1,4,6,192,768]{4,3,2,1,0:T(8,128)(2,1)} %bitcast.48, bf16[1,4,6,192,768]{4,3,2,1,0:T(8,128)(2,1)} %bitcast.47, pred[]{:T(512)S(6)} %eq.103), kind=kLoop, calls=%fused_computation.1 | loop fusion | flops 28311552 | bytes 42467328 | tf_op jit(solution)/shard_map/convert_element_type | solution.py:581
  460.1 14.4 %slice_bitcast_fusion = (f32[2,2,4,192,768]{4,3,1,2,0:T(8,128)S(1)}, f32[4,192,2,2,768]{4,1,3,0,2:T(8,128)S(1)}, f32[2,2,4,192,768]{4,3,1,2,0:T(8,128)}) fusion(f32[2,4,6,192,768]{4,3,2,1,0:T(8,128)} %fusion), kind=kLoop, calls=%fused_computation.4 | loop fusion | bytes 56623104 | tf_op jit(solution)/shard_map/transpose | solution.py:720
  474.4 4.7 copy.63
  479.1 11.4 %copy.62 = f32[4,192,2,2,768]{4,3,2,1,0:T(2,128)} copy(f32[4,192,2,2,768]{4,1,3,0,2:T(8,128)S(1)} %get-tuple-element.111) | data formatting | bytes 18874368 | tf_op jit(solution)/shard_map/transpose | solution.py:721
  490.5 12.8 %reshape.245 = f32[1,768,3072]{2,1,0:T(8,128)} reshape(f32[4,192,2,2,768]{4,3,2,1,0:T(2,128)} %copy.62) | data formatting | bytes 18874368 | tf_op jit(solution)/shard_map/reshape | solution.py:721
  503.3 4.6 copy.59
  507.9 3.8 slice_bitcast_fusion.3
  (107 shorter events, 30.7 us)
Async XLA Ops:
  7.2 5.1 copy-start
  7.2 421.9 %all-gather.4.cloned.1.call-start = ((), (), s32[]{:S(2)}) async-start(), calls=%async_computation | async-start | bytes 3194880 | tf_op jit(solution)/shard_map/all_gather | solution.py:716
  12.3 2.4 copy-start.2
  14.6 2.4 copy-start.8
  14.6 2.4 copy-start.9
  14.6 2.4 copy-start.10
  14.6 2.4 copy-start.11
  14.6 2.4 copy-start.12
  14.6 2.4 copy-start.13
  14.6 2.4 copy-start.14
  14.7 2.4 copy-start.15
  17.7 23.9 %copy-start.6 = (bf16[38,768]{1,0:T(8,128)(2,1)S(1)}, bf16[38,768]{1,0:T(8,128)(2,1)}, u32[]{:S(2)}) copy-start(bf16[38,768]{1,0:T(8,128)(2,1)} %param.26) | copy-start | bytes 175108
  17.7 23.9 %copy-start.3 = (bf16[256,768]{1,0:T(8,128)(2,1)S(1)}, bf16[256,768]{1,0:T(8,128)(2,1)}, u32[]{:S(2)}) copy-start(bf16[256,768]{1,0:T(8,128)(2,1)} %param.25) | copy-start | bytes 1179652
  37.3 15.7 %collective-permute-start = (bf16[320,768]{1,0:T(8,128)(2,1)}, bf16[320,768]{1,0:T(8,128)(2,1)S(1)}, u32[]{:S(2)}, u32[]{:S(2)}) collective-permute-start(bf16[320,768]{1,0:T(8,128)(2,1)} %front.1), channel_id=1, source_target_pairs={{0,64},{64,0},{1,65},{65,1},{2,66},{66,2},{3,67},{67,3},{4,68},{68... | collective-permute-start | bytes 1474568 | tf_op jit(solution)/shard_map/ppermute | solution.py:558
  88.4 14.5 %collective-permute-start.1 = (bf16[320,768]{1,0:T(8,128)(2,1)}, bf16[320,768]{1,0:T(8,128)(2,1)S(1)}, u32[]{:S(2)}, u32[]{:S(2)}) collective-permute-start(bf16[320,768]{1,0:T(8,128)(2,1)} %get-tuple-element.36), channel_id=1, source_target_pairs={{0,64},{64,0},{1,65},{65,1},{2,66},{66,2},{3,67},{67,3},{4,68},{68... | collective-permute-start | bytes 1474568 | tf_op jit(solution)/shard_map/ppermute | solution.py:558
  156.6 11.6 %collective-permute-start.2 = (bf16[4,1152,768]{2,1,0:T(8,128)(2,1)}, bf16[4,1152,768]{2,1,0:T(8,128)(2,1)}, u32[]{:S(2)}, u32[]{:S(2)}) collective-permute-start(bf16[4,1152,768]{2,1,0:T(8,128)(2,1)} %dynamic-slice_bitcast_fusion), channel_id=1, source_target_pairs={{0,1},{1,0},{2,3},{3,2},{4,5},{5,4},{6,7},{7,6},{8,9},{9,8},{10,11... | collective-permute-start | bytes 21233672 | tf_op jit(solution)/shard_map/ppermute | solution.py:558
  180.1 14.3 %collective-permute-start.3 = (bf16[576,768]{1,0:T(8,128)(2,1)S(1)}, bf16[576,768]{1,0:T(8,128)(2,1)S(1)}, u32[]{:S(2)}, u32[]{:S(2)}) collective-permute-start(bf16[576,768]{1,0:T(8,128)(2,1)S(1)} %get-tuple-element.119), channel_id=1, source_target_pairs={{0,8},{1,3},{2,10},{3,5},{4,12},{5,7},{6,14},{7,1},{8,16},{9,11},{... | collective-permute-start | bytes 2654216 | tf_op jit(solution)/shard_map/ppermute | solution.py:571
  181.6 13.0 %collective-permute-start.5 = (bf16[576,768]{1,0:T(8,128)(2,1)S(1)}, bf16[576,768]{1,0:T(8,128)(2,1)S(1)}, u32[]{:S(2)}, u32[]{:S(2)}) collective-permute-start(bf16[576,768]{1,0:T(8,128)(2,1)S(1)} %get-tuple-element.121), channel_id=1, source_target_pairs={{0,24},{1,7},{2,26},{3,1},{4,28},{5,3},{6,30},{7,5},{8,0},{9,15},{... | collective-permute-start | bytes 2654216 | tf_op jit(solution)/shard_map/ppermute | solution.py:571
  196.7 23.1 %collective-permute-start.6 = (bf16[1152,768]{1,0:T(8,128)(2,1)S(1)}, bf16[1152,768]{1,0:T(8,128)(2,1)S(1)}, u32[]{:S(2)}, u32[]{:S(2)}) collective-permute-start(bf16[1152,768]{1,0:T(8,128)(2,1)S(1)} %pad_maximum_fusion.1), channel_id=1, source_target_pairs={{0,24},{1,7},{2,26},{3,1},{4,28},{5,3},{6,30},{7,5},{8,0},{9,15},{... | collective-permute-start | bytes 5308424 | tf_op jit(solution)/shard_map/ppermute | solution.py:571
  201.0 24.0 %collective-permute-start.4 = (bf16[1152,768]{1,0:T(8,128)(2,1)}, bf16[1152,768]{1,0:T(8,128)(2,1)}, u32[]{:S(2)}, u32[]{:S(2)}) collective-permute-start(bf16[1152,768]{1,0:T(8,128)(2,1)} %pad_maximum_fusion), channel_id=1, source_target_pairs={{0,8},{1,3},{2,10},{3,5},{4,12},{5,7},{6,14},{7,1},{8,16},{9,11},{... | collective-permute-start | bytes 5308424 | tf_op jit(solution)/shard_map/ppermute | solution.py:571
  228.8 9.7 %collective-permute-start.7 = (bf16[288,768]{1,0:T(8,128)(2,1)}, bf16[288,768]{1,0:T(8,128)(2,1)S(1)}, u32[]{:S(2)}, u32[]{:S(2)}) collective-permute-start(bf16[288,768]{1,0:T(8,128)(2,1)} %get-tuple-element.123), channel_id=1, source_target_pairs={{0,2},{1,9},{2,4},{3,11},{4,6},{5,13},{6,0},{7,15},{8,10},{9,17},{... | collective-permute-start | bytes 1327112 | tf_op jit(solution)/shard_map/ppermute | solution.py:571
  230.4 8.5 %collective-permute-start.9 = (bf16[288,768]{1,0:T(8,128)(2,1)}, bf16[288,768]{1,0:T(8,128)(2,1)S(1)}, u32[]{:S(2)}, u32[]{:S(2)}) collective-permute-start(bf16[288,768]{1,0:T(8,128)(2,1)} %get-tuple-element.124), channel_id=1, source_target_pairs={{0,6},{1,25},{2,0},{3,27},{4,2},{5,29},{6,4},{7,31},{8,14},{9,1},{... | collective-permute-start | bytes 1327112 | tf_op jit(solution)/shard_map/ppermute | solution.py:571
  232.1 12.5 %collective-permute-start.8 = (bf16[288,768]{1,0:T(8,128)(2,1)S(1)}, bf16[288,768]{1,0:T(8,128)(2,1)S(1)}, u32[]{:S(2)}, u32[]{:S(2)}) collective-permute-start(bf16[288,768]{1,0:T(8,128)(2,1)S(1)} %get-tuple-element.125), channel_id=1, source_target_pairs={{0,4},{1,17},{2,6},{3,19},{4,0},{5,21},{6,2},{7,23},{8,12},{9,25},... | collective-permute-start | bytes 1327112 | tf_op jit(solution)/shard_map/ppermute | solution.py:571
  244.8 8.1 %collective-permute-start.10 = (bf16[144,768]{1,0:T(8,128)(2,1)S(1)}, bf16[144,768]{1,0:T(8,128)(2,1)S(1)}, u32[]{:S(2)}, u32[]{:S(2)}) collective-permute-start(bf16[144,768]{1,0:T(8,128)(2,1)S(1)} %dynamic-slice_bitcast_fusion.10), channel_id=1, source_target_pairs={{0,32},{32,0},{1,33},{33,1},{2,34},{34,2},{3,35},{35,3},{4,36},{36... | collective-permute-start | bytes 663560 | tf_op jit(solution)/shard_map/ppermute | solution.py:558
  252.9 6.0 %collective-permute-start.11 = (bf16[144,768]{1,0:T(8,128)(2,1)S(1)}, bf16[144,768]{1,0:T(8,128)(2,1)S(1)}, u32[]{:S(2)}, u32[]{:S(2)}) collective-permute-start(bf16[144,768]{1,0:T(8,128)(2,1)S(1)} %fusion.15), channel_id=1, source_target_pairs={{0,32},{32,0},{1,33},{33,1},{2,34},{34,2},{3,35},{35,3},{4,36},{36... | collective-permute-start | bytes 663560 | tf_op jit(solution)/shard_map/ppermute | solution.py:558
  259.0 8.4 %collective-permute-start.12 = (bf16[288,768]{1,0:T(8,128)(2,1)S(1)}, bf16[288,768]{1,0:T(8,128)(2,1)S(1)}, u32[]{:S(2)}, u32[]{:S(2)}) collective-permute-start(bf16[288,768]{1,0:T(8,128)(2,1)S(1)} %bitcast.149), channel_id=1, source_target_pairs={{0,6},{1,25},{2,0},{3,27},{4,2},{5,29},{6,4},{7,31},{8,14},{9,1},{... | collective-permute-start | bytes 1327112 | tf_op jit(solution)/shard_map/ppermute | solution.py:571
  260.0 9.9 %collective-permute-start.13 = (bf16[288,768]{1,0:T(8,128)(2,1)S(1)}, bf16[288,768]{1,0:T(8,128)(2,1)S(1)}, u32[]{:S(2)}, u32[]{:S(2)}) collective-permute-start(bf16[288,768]{1,0:T(8,128)(2,1)S(1)} %bitcast.150), channel_id=1, source_target_pairs={{0,4},{1,17},{2,6},{3,19},{4,0},{5,21},{6,2},{7,23},{8,12},{9,25},... | collective-permute-start | bytes 1327112 | tf_op jit(solution)/shard_map/ppermute | solution.py:571
  261.6 15.4 %collective-permute-start.14 = (bf16[288,768]{1,0:T(8,128)(2,1)S(1)}, bf16[288,768]{1,0:T(8,128)(2,1)S(1)}, u32[]{:S(2)}, u32[]{:S(2)}) collective-permute-start(bf16[288,768]{1,0:T(8,128)(2,1)S(1)} %bitcast.151), channel_id=1, source_target_pairs={{0,2},{1,9},{2,4},{3,11},{4,6},{5,13},{6,0},{7,15},{8,10},{9,17},{... | collective-permute-start | bytes 1327112 | tf_op jit(solution)/shard_map/ppermute | solution.py:571
  277.0 23.8 %collective-permute-start.16 = (bf16[1152,768]{1,0:T(8,128)(2,1)S(1)}, bf16[1152,768]{1,0:T(8,128)(2,1)S(1)}, u32[]{:S(2)}, u32[]{:S(2)}) collective-permute-start(bf16[1152,768]{1,0:T(8,128)(2,1)S(1)} %bitcast.146), channel_id=1, source_target_pairs={{0,8},{1,3},{2,10},{3,5},{4,12},{5,7},{6,14},{7,1},{8,16},{9,11},{... | collective-permute-start | bytes 5308424 | tf_op jit(solution)/shard_map/ppermute | solution.py:571
  277.3 23.6 %collective-permute-start.15 = (bf16[1152,768]{1,0:T(8,128)(2,1)S(1)}, bf16[1152,768]{1,0:T(8,128)(2,1)S(1)}, u32[]{:S(2)}, u32[]{:S(2)}) collective-permute-start(bf16[1152,768]{1,0:T(8,128)(2,1)S(1)} %bitcast.147), channel_id=1, source_target_pairs={{0,24},{1,7},{2,26},{3,1},{4,28},{5,3},{6,30},{7,5},{8,0},{9,15},{... | collective-permute-start | bytes 5308424 | tf_op jit(solution)/shard_map/ppermute | solution.py:571
  300.8 14.3 %collective-permute-start.17 = (bf16[576,768]{1,0:T(8,128)(2,1)S(1)}, bf16[576,768]{1,0:T(8,128)(2,1)S(1)}, u32[]{:S(2)}, u32[]{:S(2)}) collective-permute-start(bf16[576,768]{1,0:T(8,128)(2,1)S(1)} %slice.162), channel_id=1, source_target_pairs={{0,8},{1,3},{2,10},{3,5},{4,12},{5,7},{6,14},{7,1},{8,16},{9,11},{... | collective-permute-start | bytes 2654216 | tf_op jit(solution)/shard_map/ppermute | solution.py:571
  301.0 14.2 %collective-permute-start.18 = (bf16[576,768]{1,0:T(8,128)(2,1)S(1)}, bf16[576,768]{1,0:T(8,128)(2,1)S(1)}, u32[]{:S(2)}, u32[]{:S(2)}) collective-permute-start(bf16[576,768]{1,0:T(8,128)(2,1)S(1)} %slice.163), channel_id=1, source_target_pairs={{0,24},{1,7},{2,26},{3,1},{4,28},{5,3},{6,30},{7,5},{8,0},{9,15},{... | collective-permute-start | bytes 2654216 | tf_op jit(solution)/shard_map/ppermute | solution.py:571
  316.5 4.3 copy-start.7
  316.5 5.0 copy-start.4
  316.5 5.0 copy-start.5
  317.8 120.1 %collective-permute-start.19 = (bf16[4,1152,768]{2,1,0:T(8,128)(2,1)}, bf16[4,1152,768]{2,1,0:T(8,128)(2,1)}, u32[]{:S(2)}, u32[]{:S(2)}) collective-permute-start(bf16[4,1152,768]{2,1,0:T(8,128)(2,1)} %bitcast_dynamic-update-slice_fusion), channel_id=1, source_target_pairs={{0,1},{1,0},{2,3},{3,2},{4,5},{5,4},{6,7},{7,6},{8,9},{9,8},{10,11... | collective-permute-start | bytes 21233672 | tf_op jit(solution)/shard_map/ppermute | solution.py:558
  431.8 5.3 %collective-permute-start.20 = (f32[768]{0:T(1024)S(1)}, f32[768]{0:T(1024)S(1)}, u32[]{:S(2)}, u32[]{:S(2)}) collective-permute-start(f32[768]{0:T(1024)S(1)} %get-tuple-element.128), channel_id=1, source_target_pairs={{0,64},{64,0},{1,65},{65,1},{2,66},{66,2},{3,67},{67,3},{4,68},{68... | collective-permute-start | bytes 9224 | tf_op jit(solution)/shard_map/ppermute | solution.py:558
  507.9 3.8 copy-start.1
Sparse Core Ops, SparseCore 0:
  321.6 107.4 all-gather.3
where the time goes:
time: 525 us; the launch traced here: 519 us
  waiting for transfers between devices  238 us (45%)
  Pallas kernels  101 us (19%)
  local copies, waits for them, and re-layouts  78.3 us (15%)
  other arithmetic  50.8 us (10%)
  starting transfers between devices  34 us (6%)
  between operations  14.7 us (3%)
    all_gather x1, waiting for transfers between devices, on_device(): small_sum = jnp.sum(lax.all_gather(small, DP, axis=0), axis=0)  106 us
    ppermute x14, waiting for transfers between devices, turn(): return lax.ppermute(value, PLANE, pairs)  86.2 us
    pallas_call x1, Pallas kernels, back(): pl.pallas_call(back_kernel, out_shape=[jax.ShapeDtypeStruct((ROWS, D), WI...  46.4 us
    ppermute x7, waiting for transfers between devices, shift(): lax.ppermute(value, axis, [(i, (i + by) % size) for i in range(size)])  45.7 us
    pallas_call x1, Pallas kernels, middle(): pl.pallas_call(middle_kernel, out_shape=[jax.ShapeDtypeStruct((ROWS, D),...  34.5 us
    convert_element_type x1, other arithmetic, wide(): return value.astype(WIDE)  22.1 us
    ppermute x14, starting transfers between devices, turn(): return lax.ppermute(value, PLANE, pairs)  20.8 us
    pallas_call x1, Pallas kernels, front(): pl.pallas_call(front_kernel, out_shape=jax.ShapeDtypeStruct((ROWS, D), LO...  19.6 us
  transfers between devices with their start and end apart: 22, of which 19 were waited for; matrix products, arithmetic and copies ran while one was open for 4% of the time, Pallas kernels for 0%

commit v1 on v0

--- a/solution.py
+++ b/solution.py
@@ -19,8 +19,8 @@
 SEQ_ROWS = L + PICKS
 EPSILON = 1e-05
 SCALE = HD ** (-0.5)
-TILE = 512
-BAND = 32
+TILE = 768
+BAND = 64
 LOW = jnp.bfloat16
 WIDE = jnp.float32
 
@@ -69,27 +69,18 @@
 
 
 def bands(body):
-    def step(index, carry):
-        body(pl.ds(pl.multiple_of(index * BAND, BAND), BAND))
-        return carry
-
-    lax.fori_loop(0, ROWS // BAND, step, 0)
+    for index in range(ROWS // BAND):
+        body(slice(index * BAND, (index + 1) * BAND))
 
 
 def pairs_loop(body):
-    def step(pair, carry):
-        body(pair, pl.ds(pl.multiple_of(pair * 128, 128), 128))
-        return carry
-
-    lax.fori_loop(0, PAIRS, step, 0)
+    for pair in range(PAIRS):
+        body(pair, slice(pair * 128, (pair + 1) * 128))
 
 
 def tiles_loop(body):
-    def step(tile, carry):
-        body(pl.ds(pl.multiple_of(tile * TILE, TILE), TILE))
-        return carry
-
-    lax.fori_loop(0, FF // TILE, step, 0)
+    for tile in range(FF // TILE):
+        body(slice(tile * TILE, (tile + 1) * TILE))
 
 
 def norm_rows(values):
@@ -217,7 +208,7 @@
     bands(first_norm)
 
 
-def backward_attend(w, s, table=None):
+def backward_attend_first(w, s, table=None):
     s.dmixed[...] = nt(s.attended[...], w.out[...]).astype(LOW)
 
     def attend(pair, lanes):
@@ -241,8 +232,16 @@
             table(pair, slopes)
 
     pairs_loop(attend)
+
+
+def backward_attend_last(w, s):
     s.total[...] += nt(s.dquery[...], w.query[...])
     s.total[:CONTENT] += nt(s.dkey[...], w.key[...]) + nt(s.dvalue[...], w.value[...])
+
+
+def backward_attend(w, s, table=None):
+    backward_attend_first(w, s, table)
+    backward_attend_last(w, s)
 
 
 class Names:
@@ -326,10 +325,39 @@
     )(x, *matrices, masks, vec, b_expand)
 
 
-def middle_kernel(x, cot, *refs):
+HALF = FF // 2
+QUARTER = D // 4
+EARLY = 3 * D + HALF
+LATE = D + HALF
+PIECE = CONTENT + ROWS
+EXTRA = 32
+SMEM = pl.BlockSpec(memory_space=pltpu.SMEM)
+LATER = ("normed2", "root2", "slope", "normed1", "root1", "activated", "first_low")
+SAVED = LATER + ("probs", "query", "key", "value")
+
+
+def columns(ref, start, size):
+    return ref.at[:, pl.ds(pl.multiple_of(start, 128), size)]
+
+
+def rows_at(ref, start, size):
+    return ref.at[pl.ds(pl.multiple_of(start, 64), size)]
+
+
+def start_all(pairs, sems, base=0):
+    copies = [
+        pltpu.make_async_copy(source, target, sems.at[base + index])
+        for index, (source, target) in enumerate(pairs)
+    ]
+    for copy in copies:
+        copy.start()
+    return copies
+
+
+def middle_kernel(info, x, cot, *refs):
     matrices, (masks, vec, b_expand), rest = refs[:6], refs[6:9], refs[9:]
-    (out, grad), rest = rest[:2], rest[2:]
-    kept_out, rest = rest[: len(KEPT)], rest[len(KEPT) :]
+    (out, grad, early, pair_out), rest = rest[:4], rest[4:]
+    saved_out, rest = rest[: len(SAVED)], rest[len(SAVED) :]
     held, (mask_buf,), rest = rest[:6], rest[6:7], rest[7:]
     kept, rest = rest[: len(KEPT)], rest[len(KEPT) :]
     passed, rest = rest[: len(PASSED)], rest[len(PASSED) :]
@@ -343,25 +371,36 @@
     w = Names(**dict(zip(MATRICES, held)))
     s = Names(total=total, out=out, **dict(zip(KEPT, kept)), **dict(zip(PASSED, passed)))
     forward(x, w, vec, b_expand, mask_buf, s, True, ready)
-    done = fetcher([(n, a, b) for n, a, b in zip(KEPT, kept, kept_out)], out_sems)
+    other = 1 - info[0]
+    pairs = [
+        (x, early.at[:, :D]),
+        (s.mixed, early.at[:, D : 2 * D]),
+        (s.first_low, early.at[:, 2 * D : 3 * D]),
+        (columns(s.activated, other * HALF, HALF), early.at[:, 3 * D :]),
+        (x, pair_out.at[0]),
+        (s.mixed, pair_out.at[1]),
+    ] + [(s.__dict__[n], ref) for n, ref in zip(SAVED, saved_out)]
+    copies = start_all(pairs, out_sems)
     backward_feed(cot, w, vec, s)
     backward_expand(w, vec, s)
     backward_attend(w, s)
     grad[...] = total[...].astype(LOW)
-    for name in KEPT:
-        done(name)
-
-
-def middle(x, cot, matrices, masks, vec, b_expand):
+    for copy in copies:
+        copy.wait()
+
+
+def middle(info, x, cot, matrices, masks, vec, b_expand):
     return pl.pallas_call(
         middle_kernel,
         out_shape=[
             jax.ShapeDtypeStruct((ROWS, D), WIDE),
             jax.ShapeDtypeStruct((ROWS, D), LOW),
+            jax.ShapeDtypeStruct((ROWS, EARLY), LOW),
+            jax.ShapeDtypeStruct((2, ROWS, D), LOW),
         ]
-        + [jax.ShapeDtypeStruct(*KEPT[n]) for n in KEPT],
-        in_specs=[VMEM] * 2 + [ANY] * 7 + [VMEM] * 2,
-        out_specs=[VMEM] * 2 + [ANY] * len(KEPT),
+        + [jax.ShapeDtypeStruct(*KEPT[n]) for n in SAVED],
+        in_specs=[SMEM] + [VMEM] * 2 + [ANY] * 7 + [VMEM] * 2,
+        out_specs=[VMEM] * 2 + [ANY] * (2 + len(SAVED)),
         scratch_shapes=[pltpu.VMEM(MATRIX_SHAPES[n], LOW) for n in MATRICES]
         + [pltpu.VMEM(MASK_SHAPE, WIDE)]
         + [pltpu.VMEM(*KEPT[n]) for n in KEPT]
@@ -369,144 +408,394 @@
         + [
             pltpu.VMEM((ROWS, D), WIDE),
             pltpu.SemaphoreType.DMA((7,)),
-            pltpu.SemaphoreType.DMA((len(KEPT),)),
+            pltpu.SemaphoreType.DMA((6 + len(SAVED),)),
         ],
         compiler_params=pltpu.CompilerParams(vmem_limit_bytes=LIMIT),
         name="middle",
-    )(x, cot, *matrices, masks, vec, b_expand)
-
-
-QUARTER = D // 4
-BLOCKS = 6
-
-
-def back_kernel(x, upper, spread, *refs):
-    matrices, (vec,), rest = refs[:6], refs[6:7], refs[7:]
-    kept_in, rest = rest[: len(KEPT)], rest[len(KEPT) :]
-    (grad, small, table, groups), rest = rest[:4], rest[4:]
-    held, rest = rest[:6], rest[6:]
-    kept, rest = rest[: len(KEPT)], rest[len(KEPT) :]
-    passed, rest = rest[: len(PASSED)], rest[len(PASSED) :]
-    total, stage, sems, out_sems = rest
-    first = ("normed2", "root2", "activated")
-    later = [n for n in KEPT if n not in first]
-    kept_pairs = {n: (n, a, b) for n, a, b in zip(KEPT, kept_in, kept)}
-    matrix_pairs = {n: ("w_" + n, a, b) for n, a, b in zip(MATRICES, matrices, held)}
-    ready = fetcher(
-        [kept_pairs[n] for n in first]
-        + [matrix_pairs["contract"], kept_pairs["slope"], matrix_pairs["expand"]]
-        + [kept_pairs[n] for n in later if n != "slope"]
-        + [matrix_pairs[n] for n in ("out", "query", "key", "value")],
-        sems,
-    )
-    w = Names(**dict(zip(MATRICES, held)))
-    s = Names(total=total, **dict(zip(KEPT, kept)), **dict(zip(PASSED, passed)))
+    )(info, x, cot, *matrices, masks, vec, b_expand)
+
+
+def feed_back_kernel(info, upper, vec, *refs):
+    names = ("normed2", "root2", "contract", "slope", "expand", "normed1", "root1")
+    sources, rest = refs[:7], refs[7:]
+    (total, branch, attended, small, own, late), rest = rest[:6], rest[6:]
+    held, (expanded, sems, out_sems) = rest[:7], rest[7:]
+    ready = fetcher(list(zip(names, sources, held)), sems)
+    buffers = dict(zip(names, held))
+    w = Names(contract=buffers["contract"], expand=buffers["expand"])
+    s = Names(
+        total=total,
+        branch=branch,
+        attended=attended,
+        expanded=expanded,
+        **{n: buffers[n] for n in ("normed2", "root2", "slope", "normed1", "root1")},
+    )
     small[...] = jnp.zeros_like(small)
 
     def sums(band, place, value):
         small[place : place + 1, :] += jnp.sum(value, axis=0, keepdims=True)
 
-    for name in first:
+    ready("normed2")
+    ready("root2")
+    backward_feed(upper, w, vec, s, sums)
+    copies = start_all([(branch, late.at[:, :D])], out_sems)
+    for name in names[2:]:
         ready(name)
-    backward_feed(upper, w, vec, s, sums)
-
-    pending = []
-
-    def emit(core, quarter, block, value):
-        slot = len(pending) % 2
-        if len(pending) >= 2:
-            pending[-2].wait()
-        stage[slot] = value.astype(LOW)
-        copy = pltpu.make_async_copy(
-            stage.at[slot], groups.at[core, quarter, block], out_sems.at[slot]
-        )
-        copy.start()
-        pending.append(copy)
-
-    for index in range(FF // QUARTER):
-        core, block, quarter = index // 8, index // 4 % 2, index % 4
-        emit(
-            core,
-            quarter,
-            block,
-            tn(s.activated[:, index * QUARTER : (index + 1) * QUARTER], s.branch[...]),
-        )
 
     def tile_sums(tile, value):
-        pass
-
-    ready("w_contract")
-    ready("slope")
-    ready("w_expand")
-    for name in later:
-        if name != "slope":
-            ready(name)
+        place = 5 + tile.start // D
+        small[place : place + 1, :] = jnp.sum(value.astype(WIDE), axis=0, keepdims=True)
+        if tile.stop == FF:
+            mine = info[0]
+            copies.extend(
+                start_all(
+                    [
+                        (columns(expanded, mine * HALF, HALF), own),
+                        (columns(expanded, (1 - mine) * HALF, HALF), late.at[:, D:]),
+                    ],
+                    out_sems,
+                    1,
+                )
+            )
+
     backward_expand(w, vec, s, sums, tile_sums)
-    for column in range(4):
-        part = jnp.sum(s.expanded[:, column * D : (column + 1) * D].astype(WIDE), axis=0, keepdims=True)
-        small[5 + column : 6 + column, :] = part
-        for quarter in range(4):
-            emit(
-                column // 2,
-                quarter,
-                2 + column % 2,
-                tn(
-                    s.first_low[:, quarter * QUARTER : (quarter + 1) * QUARTER],
-                    s.expanded[:, column * D : (column + 1) * D],
-                ),
+    for copy in copies:
+        copy.wait()
+
+
+def feed_back(info, upper, vec, matrices, saved):
+    shapes = [KEPT["normed2"], KEPT["root2"], (MATRIX_SHAPES["contract"], LOW), KEPT["slope"]]
+    shapes += [(MATRIX_SHAPES["expand"], LOW), KEPT["normed1"], KEPT["root1"]]
+    return pl.pallas_call(
+        feed_back_kernel,
+        out_shape=[
+            jax.ShapeDtypeStruct((ROWS, D), WIDE),
+            jax.ShapeDtypeStruct((ROWS, D), LOW),
+            jax.ShapeDtypeStruct((ROWS, D), LOW),
+            jax.ShapeDtypeStruct((16, D), WIDE),
+            jax.ShapeDtypeStruct((ROWS, HALF), LOW),
+            jax.ShapeDtypeStruct((ROWS, LATE), LOW),
+        ],
+        in_specs=[SMEM] + [VMEM] * 2 + [ANY] * 7,
+        out_specs=[VMEM] * 4 + [ANY] * 2,
+        scratch_shapes=[pltpu.VMEM(*shape) for shape in shapes]
+        + [
+            pltpu.VMEM((ROWS, FF), LOW),
+            pltpu.SemaphoreType.DMA((7,)),
+            pltpu.SemaphoreType.DMA((3,)),
+        ],
+        compiler_params=pltpu.CompilerParams(vmem_limit_bytes=LIMIT),
+        name="feed_back",
+    )(
+        info,
+        upper,
+        vec,
+        saved["normed2"],
+        saved["root2"],
+        matrices[5],
+        saved["slope"],
+        matrices[4],
+        saved["normed1"],
+        saved["root1"],
+    )
+
+
+def feed_grads_kernel(info, act, first_low, branch, own, early, late, *refs):
+    outs, (a_act, a_first, b_branch, b_own, stage, sems, out_sems) = refs[:8], refs[8:]
+    core, place = info[0], info[1]
+    copies = start_all(
+        [
+            (columns(act, core * HALF, HALF), a_act.at[:ROWS]),
+            (early.at[:, 3 * D :], a_act.at[ROWS:]),
+            (branch, b_branch.at[:ROWS]),
+            (late.at[:, :D], b_branch.at[ROWS:]),
+            (first_low, a_first.at[:ROWS]),
+            (early.at[:, 2 * D : 3 * D], a_first.at[ROWS:]),
+            (own, b_own.at[:ROWS]),
+            (late.at[:, D:], b_own.at[ROWS:]),
+        ],
+        sems,
+    )
+    sent = []
+
+    def send(block):
+        for k in range(4):
+            quarter = lax.rem(place + k, 4)
+            sent.extend(
+                start_all(
+                    [
+                        (
+                            rows_at(stage.at[block], quarter * QUARTER, QUARTER),
+                            outs[2 * k + block // 2].at[
+                                block % 2 * QUARTER : (block % 2 + 1) * QUARTER
+                            ],
+                        )
+                    ],
+                    out_sems,
+                    block * 4 + k,
+                )
             )
-    for name in ("out", "query", "key", "value"):
-        ready("w_" + name)
+
+    for copy in copies[:4]:
+        copy.wait()
+    for block in range(2):
+        for part in range(3):
+            start = block * D + part * 256
+            stage[block, part * 256 : (part + 1) * 256] = tn(
+                a_act[:, start : start + 256], b_branch[...]
+            ).astype(LOW)
+        send(block)
+    for copy in copies[4:]:
+        copy.wait()
+    for block in range(2):
+        for part in range(3):
+            stage[2 + block, part * 256 : (part + 1) * 256] = tn(
+                a_first[:, part * 256 : (part + 1) * 256], b_own[:, block * D : (block + 1) * D]
+            ).astype(LOW)
+        send(2 + block)
+    for copy in sent:
+        copy.wait()
+
+
+def feed_grads(info, act, first_low, branch, own, early, late):
+    return pl.pallas_call(
+        feed_grads_kernel,
+        out_shape=[jax.ShapeDtypeStruct((2 * QUARTER, D), LOW)] * 8,
+        in_specs=[SMEM] + [ANY] * 6,
+        out_specs=[ANY] * 8,
+        scratch_shapes=[
+            pltpu.VMEM((2 * ROWS, HALF), LOW),
+            pltpu.VMEM((2 * ROWS, D), LOW),
+            pltpu.VMEM((2 * ROWS, D), LOW),
+            pltpu.VMEM((2 * ROWS, HALF), LOW),
+            pltpu.VMEM((4, D, D), LOW),
+            pltpu.SemaphoreType.DMA((8,)),
+            pltpu.SemaphoreType.DMA((16,)),
+        ],
+        compiler_params=pltpu.CompilerParams(vmem_limit_bytes=LIMIT),
+        name="feed_grads",
+    )(info, act, first_low, branch, own, early, late)
+
+
+def attend_back_kernel(info, total_in, attended, small_in, spread, output, *refs):
+    names = ("out", "value", "probs", "key", "query", "w_query", "w_key", "w_value")
+    sources, rest = refs[:8], refs[8:]
+    (content_ends, query_ends, small, table, own, send), rest = rest[:6], rest[6:]
+    held, (total, dmixed, pieces, sems, out_sems) = rest[:8], rest[8:]
+    ready = fetcher(list(zip(names, sources, held)), sems)
+    buffers = dict(zip(names, held))
+    w = Names(out=buffers["out"], query=buffers["w_query"], key=buffers["w_key"])
+    w.value = buffers["w_value"]
+    s = Names(
+        total=total,
+        attended=attended,
+        dmixed=dmixed,
+        dquery=pieces.at[0, :ROWS],
+        dkey=pieces.at[0, ROWS:],
+        dvalue=pieces.at[1, ROWS:],
+        **{n: buffers[n] for n in ("probs", "query", "key", "value")},
+    )
+    total[...] = total_in[...]
+    pieces[1, :ROWS] = attended[...]
 
     def table_sum(pair, slopes):
-        both = jnp.concatenate([slope[:SEQ_ROWS] for slope in slopes])
-        table[2 * pair] = nn(spread[...], both)
-        both = jnp.concatenate([slope[SEQ_ROWS:] for slope in slopes])
-        table[2 * pair + 1] = nn(spread[...], both)
-
-    backward_attend(w, s, table_sum)
-    grad[...] = total[...]
+        for odd in range(2):
+            both = jnp.concatenate(
+                [slope[odd * SEQ_ROWS : (odd + 1) * SEQ_ROWS] for slope in slopes]
+            )
+            table[2 * pair + odd] = nn(spread[...], both)
+
+    for name in names:
+        ready(name)
+    backward_attend_first(w, s, table_sum)
+    copies = start_all([(pieces.at[info[0]], own), (pieces.at[1 - info[0]], send)], out_sems)
+    small[...] = small_in[...]
     small[0:1, :] = jnp.sum(s.dquery[...].astype(WIDE), axis=0, keepdims=True)
     small[1:2, :] = jnp.sum(s.dvalue[...].astype(WIDE), axis=0, keepdims=True)
-    for number, (former, latter) in enumerate(
-        ((x, s.dquery), (x, s.dkey), (x, s.dvalue), (s.mixed, s.attended))
-    ):
-        count = latter.shape[0]
-        for quarter in range(4):
-            emit(
-                number // 2,
-                quarter,
-                4 + number % 2,
-                tn(former[:count, quarter * QUARTER : (quarter + 1) * QUARTER], latter[...]),
-            )
-    pending[-2].wait()
-    pending[-1].wait()
-
-
-def back(x, upper, spread, matrices, vec, kept):
-    copies = len(KEPT) + len(MATRICES)
+    backward_attend_last(w, s)
+    first = info[2] == 1
+    content_ends[...] = jnp.where(first, total[:CONTENT], output[:CONTENT])
+    picks = query_ends.shape[0] // SEQS
+    for seq in range(SEQS):
+        band = slice(CONTENT + seq * PICKS, CONTENT + seq * PICKS + picks)
+        query_ends[seq * picks : (seq + 1) * picks] = jnp.where(first, total[band], output[band])
+    for copy in copies:
+        copy.wait()
+
+
+def attend_back(info, total, attended, small, spread, output, matrices, saved, picks):
+    sources = [matrices[3], saved["value"], saved["probs"], saved["key"], saved["query"]]
+    sources += [matrices[0], matrices[1], matrices[2]]
     return pl.pallas_call(
-        back_kernel,
+        attend_back_kernel,
         out_shape=[
-            jax.ShapeDtypeStruct((ROWS, D), WIDE),
+            jax.ShapeDtypeStruct((CONTENT, D), WIDE),
+            jax.ShapeDtypeStruct((SEQS * picks, D), WIDE),
             jax.ShapeDtypeStruct((16, D), WIDE),
             jax.ShapeDtypeStruct((H, L, L), WIDE),
-            jax.ShapeDtypeStruct((2, 4, BLOCKS, QUARTER, D), LOW),
+            jax.ShapeDtypeStruct((PIECE, D), LOW),
+            jax.ShapeDtypeStruct((PIECE, D), LOW),
         ],
-        in_specs=[VMEM] * 3 + [ANY] * 6 + [VMEM] + [ANY] * len(KEPT),
-        out_specs=[VMEM] * 3 + [ANY],
-        scratch_shapes=[pltpu.VMEM(MATRIX_SHAPES[n], LOW) for n in MATRICES]
-        + [pltpu.VMEM(*KEPT[n]) for n in KEPT]
-        + [pltpu.VMEM(*PASSED[n]) for n in PASSED]
+        in_specs=[SMEM] + [VMEM] * 5 + [ANY] * 8,
+        out_specs=[VMEM] * 4 + [ANY] * 2,
+        scratch_shapes=[pltpu.VMEM(ref.shape, LOW) for ref in sources]
         + [
             pltpu.VMEM((ROWS, D), WIDE),
-            pltpu.VMEM((2, QUARTER, D), LOW),
-            pltpu.SemaphoreType.DMA((copies,)),
+            pltpu.VMEM((ROWS, D), LOW),
+            pltpu.VMEM((2, PIECE, D), LOW),
+            pltpu.SemaphoreType.DMA((8,)),
             pltpu.SemaphoreType.DMA((2,)),
         ],
         compiler_params=pltpu.CompilerParams(vmem_limit_bytes=LIMIT),
-        name="back",
-    )(x, upper, spread, *matrices, vec, *kept)
+        name="attend_back",
+    )(info, total, attended, small, spread, output, *sources)
+
+
+def attend_grads_kernel(info, pair, early, own, arrived, small, *refs):
+    outs, rest = refs[:8], refs[8:]
+    a_rows, a_content, b_rows, b_content, stage, extra, sems, out_sems = rest
+    core, place = info[0], info[1]
+    copies = start_all(
+        [
+            (pair.at[core], a_rows.at[:ROWS]),
+            (columns(early, core * D, D), a_rows.at[ROWS:]),
+            (own.at[:ROWS], b_rows.at[:ROWS]),
+            (arrived.at[:ROWS], b_rows.at[ROWS:]),
+            (pair.at[0, :CONTENT], a_content.at[:CONTENT]),
+            (early.at[:CONTENT, :D], a_content.at[CONTENT:]),
+            (own.at[ROWS:], b_content.at[:CONTENT]),
+            (arrived.at[ROWS:], b_content.at[CONTENT:]),
+        ],
+        sems,
+    )
+    extra[...] = jnp.zeros_like(extra)
+    part = small[pl.ds(pl.multiple_of(core * 8, 8), 8), :]
+    extra[0] = jnp.concatenate([part, jnp.zeros((EXTRA - 8, D), WIDE)]).astype(LOW)
+    sent = []
+    for block, (former, latter) in enumerate(((a_rows, b_rows), (a_content, b_content))):
+        for copy in copies[4 * block : 4 * block + 4]:
+            copy.wait()
+        for part in range(3):
+            stage[block, part * 256 : (part + 1) * 256] = tn(
+                former[:, part * 256 : (part + 1) * 256], latter[...]
+            ).astype(LOW)
+        for k in range(4):
+            quarter = lax.rem(place + k, 4)
+            target = outs[2 * k + block]
+            sent.extend(
+                start_all(
+                    [
+                        (rows_at(stage.at[block], quarter * QUARTER, QUARTER), target.at[:QUARTER]),
+                        (extra.at[block], target.at[QUARTER:]),
+                    ],
+                    out_sems,
+                    block * 8 + 2 * k,
+                )
+            )
+    for copy in sent:
+        copy.wait()
+
+
+def attend_grads(info, pair, early, own, arrived, small):
+    return pl.pallas_call(
+        attend_grads_kernel,
+        out_shape=[jax.ShapeDtypeStruct((QUARTER + EXTRA, D), LOW)] * 8,
+        in_specs=[SMEM] + [ANY] * 4 + [VMEM],
+        out_specs=[ANY] * 8,
+        scratch_shapes=[
+            pltpu.VMEM((2 * ROWS, D), LOW),
+            pltpu.VMEM((2 * CONTENT, D), LOW),
+            pltpu.VMEM((2 * ROWS, D), LOW),
+            pltpu.VMEM((2 * CONTENT, D), LOW),
+            pltpu.VMEM((2, D, D), LOW),
+            pltpu.VMEM((2, EXTRA, D), LOW),
+            pltpu.SemaphoreType.DMA((8,)),
+            pltpu.SemaphoreType.DMA((16,)),
+        ],
+        compiler_params=pltpu.CompilerParams(vmem_limit_bytes=LIMIT),
+        name="attend_grads",
+    )(info, pair, early, own, arrived, small)
+
+
+def spread_kernel(targets, keys, count, info, *refs):
+    pieces = refs[: len(keys)]
+    outs = refs[len(refs) - 2 * len(keys) - 2 - count : len(refs) - 2 * len(keys) - 2]
+    held = refs[len(refs) - 2 * len(keys) - 2 : len(refs) - len(keys) - 2]
+    wide_held = refs[len(refs) - len(keys) - 2 : len(refs) - 2]
+    sems, out_sems = refs[-2:]
+    copies = start_all(list(zip(pieces, held)), sems)
+    finish = []
+    for index, (sibling, k, half) in enumerate(keys):
+        core = 1 - info[0] if sibling else info[0]
+        quarter = lax.rem((info[3] if sibling else info[1]) + k, 4)
+        copies[index].wait()
+        wide_held[index][...] = held[index][...].astype(WIDE)
+        finish.append(targets(outs, wide_held[index], half, core, quarter, out_sems, index))
+    for action in finish:
+        action()
+
+
+def feed_targets(outs, source, half, core, quarter, sems, index):
+    copies = []
+    for block in range(2):
+        part = source.at[block * QUARTER : (block + 1) * QUARTER]
+        if half == 0:
+            target = rows_at(outs[0], core * HALF + block * D + quarter * QUARTER, QUARTER)
+        else:
+            target = columns(
+                rows_at(outs[1], quarter * QUARTER, QUARTER), (core * 2 + block) * D, D
+            )
+        copies.append((part, target))
+    copies = start_all(copies, sems, 2 * index)
+
+    def finish():
+        for copy in copies:
+            copy.wait()
+
+    return finish
+
+
+def attend_targets(outs, source, half, core, quarter, sems, index):
+    part = source.at[:QUARTER]
+    copies = [
+        pltpu.make_async_copy(
+            part, rows_at(outs[2 * number + half], quarter * QUARTER, QUARTER), sems.at[2 * index]
+        )
+        for number in range(2)
+    ]
+    for number in range(2):
+        pl.when(core == number)(copies[number].start)
+
+    def finish():
+        for number in range(2):
+            pl.when(core == number)(copies[number].wait)
+
+    return finish
+
+
+def spread_pieces(targets, shapes, info, pieces, outs, name):
+    keys = tuple(pieces)
+    arrays = [pieces[key] for key in keys]
+    given = list(outs or ())
+
+    def kernel(*refs):
+        spread_kernel(targets, keys, len(shapes), *refs)
+
+    return pl.pallas_call(
+        kernel,
+        out_shape=[jax.ShapeDtypeStruct(shape, WIDE) for shape in shapes],
+        in_specs=[SMEM] + [ANY] * (len(keys) + len(given)),
+        out_specs=[ANY] * len(shapes),
+        scratch_shapes=[pltpu.VMEM(array.shape, LOW) for array in arrays]
+        + [pltpu.VMEM(array.shape, WIDE) for array in arrays]
+        + [pltpu.SemaphoreType.DMA((len(keys),)), pltpu.SemaphoreType.DMA((2 * len(keys),))],
+        input_output_aliases={1 + len(keys) + i: i for i in range(len(given))},
+        compiler_params=pltpu.CompilerParams(vmem_limit_bytes=LIMIT),
+        cost_estimate=pl.CostEstimate(
+            flops=0, bytes_accessed=sum(array.size * 6 for array in arrays), transcendentals=0
+        ),
+        name=name,
+    )(info, *arrays, *given)
 
 
 LIMITS = (12, 16, 23, 32, 46, 64, 91)
@@ -585,74 +874,60 @@
     return lax.dynamic_index_in_dim(parts, index, 0, keepdims=False)
 
 
-def ring_reduce(parts, outer):
-    me = place(outer)
-    own, after, across, before = (pick(parts, (me + k) % 4) for k in range(4))
-    half = parts.shape[1] // 2
-    from_left = turn(across[:half], outer, 1)
-    from_right = turn(across[half:], outer, -1)
-    to_right = jnp.concatenate(
-        [(wide(after[:half]) + wide(from_left)).astype(LOW), after[half:]]
-    )
-    to_left = jnp.concatenate(
-        [before[:half], (wide(before[half:]) + wide(from_right)).astype(LOW)]
-    )
-    left_sum = turn(to_right, outer, 1)
-    right_sum = turn(to_left, outer, -1)
-    return (wide(own) + wide(left_sum) + wide(right_sum)).astype(LOW)
-
-
-def direct_reduce(parts, outer):
-    me = place(outer)
-    total = wide(pick(parts, me))
-    for by in (1, 2, -1):
-        total += wide(turn(pick(parts, (me + by) % 4), outer, by))
-    return total.astype(LOW)
-
-
-def join(parts, outer):
-    me = place(outer)
-    whole = jnp.zeros((4,) + parts[0].shape, parts[0].dtype)
-    for k, part in enumerate(parts):
-        whole = lax.dynamic_update_index_in_dim(whole, part, (me + k) % 4, 0)
-    return whole
-
-
-def ring_gather(own, outer):
-    half = own.shape[0] // 2
-    before = turn(own, outer, 1)
-    after = turn(own, outer, -1)
-    across = jnp.concatenate([turn(before[:half], outer, 1), turn(after[half:], outer, -1)])
-    return join((own, after, across, before), outer)
-
-
-def direct_gather(own, outer):
-    after, across, before = (turn(own, outer, by) for by in (-1, 2, 1))
-    return join((own, after, across, before), outer)
-
-
-def pair_reduce(parts, axis):
-    me = lax.axis_index(axis)
-    arrived = shift(pick(parts, 1 - me), axis, 1)
-    return (wide(pick(parts, me)) + wide(arrived)).astype(LOW)
-
-
-def pair_gather(own, axis):
-    me = lax.axis_index(axis)
-    arrived = shift(own, axis, 1)
-    return jnp.where(me == 0, jnp.stack([own, arrived]), jnp.stack([arrived, own]))
-
-
-def reduce_groups(groups):
-    count = BLOCKS * QUARTER
-    part = pair_reduce(groups.reshape(2, 4, count, D), "c")
-    part = ring_reduce(part, True)
-    part = direct_reduce(part.reshape(4, count // 4, D), False)
-    part = pair_reduce(part.reshape(2, count // 8, D), "z")
-    part = pair_gather(part, "z").reshape(count // 4, D)
-    part = direct_gather(part, False).reshape(count, D)
-    part = ring_gather(part, True)
-    return pair_gather(part, "c").reshape(2, 4, BLOCKS, QUARTER, D)
+def total_of(*terms):
+    return sum(wide(term) for term in terms).astype(LOW)
+
+
+def chain_reduce(terms):
+    (own0, own1), (after0, after1), (across0, across1), (before0, before1) = terms
+    far0 = turn(across0, True, 1)
+    far1 = turn(across1, True, -1)
+    left1 = turn(after1, True, 1)
+    right0 = turn(before0, True, -1)
+    left0 = turn(total_of(after0, far0), True, 1)
+    right1 = turn(total_of(before1, far1), True, -1)
+    sums = [total_of(own0, left0, right0), total_of(own1, left1, right1)]
+    count = own0.shape[0] // 4
+    parts = jnp.concatenate([part.reshape(4, count, D) for part in sums], axis=1)
+    me = place(False)
+    arrived = [turn(pick(parts, (me + by) % 4), False, by) for by in (1, 2, -1)]
+    part = total_of(pick(parts, me), *arrived).reshape(2, count, D)
+    me = lax.axis_index("z")
+    return total_of(pick(part, me), shift(pick(part, 1 - me), "z", 1))
+
+
+def chain_gather(part):
+    count = part.shape[0]
+    arrived = shift(part, "z", 1)
+    low = lax.axis_index("z") == 0
+    part = jnp.concatenate([jnp.where(low, part, arrived), jnp.where(low, arrived, part)])
+    me = place(False)
+    whole = jnp.zeros((4, 2 * count, D), LOW)
+    for k, piece in enumerate([part] + [turn(part, False, -by) for by in (1, 2, -1)]):
+        whole = lax.dynamic_update_index_in_dim(whole, piece, (me + k) % 4, 0)
+    own = [whole[:, half * count : (half + 1) * count].reshape(4 * count, D) for half in range(2)]
+    pieces = {(0, 0): own[0], (0, 1): own[1]}
+    pieces[3, 0] = turn(own[0], True, 1)
+    pieces[1, 1] = turn(own[1], True, -1)
+    pieces[3, 1] = turn(own[1], True, 1)
+    pieces[1, 0] = turn(own[0], True, -1)
+    pieces[2, 0] = turn(pieces[3, 0], True, 1)
+    pieces[2, 1] = turn(pieces[1, 1], True, -1)
+    near = {(0,) + key: piece for key, piece in pieces.items()}
+    far = {(1,) + key: shift(piece, "c", 1) for key, piece in pieces.items()}
+    return near | far
+
+
+def settle(targets, shapes, info, pieces, name):
+    outs = None
+    for last in (False, True):
+        some = {key: piece for key, piece in pieces.items() if (key[1] == 2) == last}
+        outs = spread_pieces(targets, shapes, info, some, outs, name + "_" + "ab"[last])
+    return outs
+
+
+def send(value, by):
+    return lax.ppermute(value, "s", [(0, 1)] if by > 0 else [(1, 0)])
 
 
 def on_device(
@@ -702,40 +977,58 @@
         [b_query, b_value, b_out, norm1_gain, norm1_bias, b_contract, norm2_gain, norm2_bias]
     )
     b_expand = b_expand[None]
+    core = lax.axis_index("c")
+    info = jnp.stack([core, place(True), is_first.astype(jnp.int32), place(False)])
     first_out = front(own_rows, matrices, masks, vec, b_expand)
-    rows = jnp.where(is_first, own_rows, shift(first_out, "s", 1))
-    output, rows_grad, *kept = middle(rows, cotangent, matrices, masks, vec, b_expand)
-    upper = jnp.where(is_first, shift(rows_grad, "s", 1), cotangent)
-    rows_grad, small, slopes, groups = back(rows, upper, spread, matrices, vec, kept)
-    ends = jnp.where(is_first, rows_grad, output)
-    content_ends = ends[None, :CONTENT]
-    query_ends = ends[CONTENT:].reshape(SEQS, PICKS, D)[:, :picks].reshape(1, SEQS * picks, D)
+    rows = jnp.where(is_first, own_rows, send(first_out, 1))
+    output, rows_grad, early, pair, *kept = middle(
+        info, rows, cotangent, matrices, masks, vec, b_expand
+    )
+    saved = dict(zip(SAVED, kept))
+    upper = jnp.where(is_first, send(rows_grad, -1), cotangent)
+    early = shift(early, "c", 1)
+    total, branch, attended, small, own, late = feed_back(info, upper, vec, matrices, saved)
+    late = shift(late, "c", 1)
+    terms = feed_grads(info, saved["activated"], saved["first_low"], branch, own, early, late)
+    feed_part = chain_reduce([terms[2 * k : 2 * k + 2] for k in range(4)])
+    content_ends, query_ends, small, slopes, own, pass_on = attend_back(
+        info, total, attended, small, spread, output, matrices, saved, picks
+    )
+    arrived = shift(pass_on, "c", 1)
     table = jnp.einsum("krl,hrl->kh", diagonals(), slopes, precision=TOP_PRECISION)
     table = jnp.pad(table.reshape(1, NB * H), ((0, 0), (0, D - NB * H)))
-    small = jnp.concatenate([small[:12], table])
-    small_sum = jnp.sum(lax.all_gather(small, DP, axis=0), axis=0)
-    table_row = small_sum[12]
-    table_total = (table_row + shift(table_row, "s", 1))[: NB * H].reshape(NB, H)
-    groups = wide(reduce_groups(groups))
-    contract = groups[:, :, 0:2].transpose(0, 2, 1, 3, 4).reshape(1, FF, D)
-    expand = groups[:, :, 2:4].transpose(1, 3, 0, 2, 4).reshape(1, D, FF)
-    heads = groups[:, :, 4:6].transpose(0, 2, 1, 3, 4).reshape(4, 1, D, D)
+    small = jnp.concatenate([small[:12], table, small[13:]])
+    small = small + shift(small, "c", 1)
+    small = jnp.concatenate([small[:12], small[12:] + shift(small[12:], "s", 1)])
+    terms = attend_grads(info, pair, early, own, arrived, small)
+    attend_part = chain_reduce([terms[2 * k : 2 * k + 2] for k in range(4)])
+    feed_pieces = chain_gather(feed_part)
+    attend_pieces = chain_gather(attend_part)
+    contract, expand = settle(feed_targets, ((FF, D), (D, FF)), info, feed_pieces, "feed_out")
+    g_query, g_key, g_out, g_value = settle(
+        attend_targets, ((D, D),) * 4, info, attend_pieces, "attend_out"
+    )
+    mine, other = (attend_pieces[far, 0, 0][QUARTER : QUARTER + 8] for far in (0, 1))
+    small_sum = wide(
+        jnp.concatenate([jnp.where(core == 0, mine, other), jnp.where(core == 0, other, mine)])
+    )
+    table_total = small_sum[12, : NB * H].reshape(NB, H)
     row = lambda k: small_sum[k][None]
     return (
-        content_ends,
-        query_ends,
-        heads[0],
+        content_ends[None],
+        query_ends[None],
+        g_query[None],
         row(0),
-        heads[1],
-        heads[2],
+        g_key[None],
+        g_value[None],
         row(1),
-        heads[3],
+        g_out[None],
         row(2),
         row(3),
         row(4),
-        expand,
+        expand[None],
         small_sum[5:9].reshape(1, FF),
-        contract,
+        contract[None],
         row(9),
         row(10),
         row(11),

time: 525 us -> 307 us (0.58)
  waiting for transfers between devices: 238 us -> 92.1 us
  local copies, waits for them, and re-layouts: 78.3 us -> 11.6 us
  starting transfers between devices: 34 us -> 73.4 us
  other arithmetic: 50.8 us -> 17 us
  between operations: 14.7 us -> 2.11 us
    all_gather x1 -> x0, waiting for transfers between devices: 106 us -> none  [on_device(): small_sum = jnp.sum(lax.all_gather(small, DP, axis=0), axis=0)]
    ppermute x14 -> x36, starting transfers between devices: 20.8 us -> 57.5 us  [turn(): return lax.ppermute(value, PLANE, pairs)]
    transpose x4 -> x0, local copies, waits for them, and re-layouts: 35 us -> none  [the longest x2 19.1 us: on_device(): contract = groups[:, :, 0:2].transpose(0, 2, 1, 3, 4).reshape(1, FF, D)]
    ppermute x14 -> x36, waiting for transfers between devices: 86.2 us -> 53.7 us  [turn(): return lax.ppermute(value, PLANE, pairs)]
    ppermute x7 -> x25, waiting for transfers between devices: 45.7 us -> 15 us  [shift(): lax.ppermute(value, axis, [(i, (i + by) % size) for i in range(size)])]
    ppermute x0 -> x2, waiting for transfers between devices: none -> 23.4 us  [send(): return lax.ppermute(value, 's', [(0, 1)] if by > 0 else [(1, 0)])]
    convert_element_type x1, other arithmetic: 22.1 us -> 0.73 us  [wide(): return value.astype(WIDE)]
    reshape x2 -> x0, local copies, waits for them, and re-layouts: 13.6 us -> none  [the longest x1 12.8 us: on_device(): expand = groups[:, :, 2:4].transpose(1, 3, 0, 2, 4).reshape(1, D, FF)]
  transfers between devices with their start and end apart: 22 -> 63, of which waited for: 19 -> 23; matrix products, arithmetic and copies ran while one was open for 4% -> 6% of each run, Pallas kernels for 0% -> 18%
where the time goes in v1:
time: 307 us; the launch traced here: 302 us
  Pallas kernels  102 us (33%)
  waiting for transfers between devices  92.1 us (30%)
  starting transfers between devices  73.4 us (24%)
  other arithmetic  17 us (6%)
  local copies, waits for them, and re-layouts  11.6 us (4%)
  matrix products  3.75 us (1%)
    ppermute x36, starting transfers between devices, turn(): return lax.ppermute(value, PLANE, pairs)  57.5 us
    ppermute x36, waiting for transfers between devices, turn(): return lax.ppermute(value, PLANE, pairs)  53.7 us
    pallas_call x1, Pallas kernels, middle(): pl.pallas_call(middle_kernel, out_shape=[jax.ShapeDtypeStruct((ROWS, D),...  32.9 us
    ppermute x2, waiting for transfers between devices, send(): return lax.ppermute(value, 's', [(0, 1)] if by > 0 else [(1, 0)])  23.4 us
    pallas_call x4, Pallas kernels, spread_pieces(): pl.pallas_call(kernel, out_shape=[jax.ShapeDtypeStruct(shape, WIDE) for s...  20 us
    ppermute x25, waiting for transfers between devices, shift(): lax.ppermute(value, axis, [(i, (i + by) % size) for i in range(size)])  15 us
    pallas_call x1, Pallas kernels, attend_back(): pl.pallas_call(attend_back_kernel, out_shape=[jax.ShapeDtypeStruct((CONTE...  12.4 us
    pallas_call x1, Pallas kernels, feed_back(): pl.pallas_call(feed_back_kernel, out_shape=[jax.ShapeDtypeStruct((ROWS, D...  11.7 us
  transfers between devices with their start and end apart: 63, of which 23 were waited for; matrix products, arithmetic and copies ran while one was open for 6% of the time, Pallas kernels for 18%

profile of v1, /device:TPU:0, one launch (start us, length us, event | category | flops | bytes accessed | tf_op | source)
XLA Modules:
  0.0 301.8 jit_solution(7190954629266544074)
XLA Ops:
  4.9 1.7 select_bitcast_fusion
  10.7 11.4 %front.1 = bf16[320,768]{1,0:T(8,128)(2,1)} custom-call(bf16[320,768]{1,0:T(8,128)(2,1)} %pad_maximum_fusion.x, bf16[768,768]{1,0:T(8,128)(2,1)} %bitcast.109, bf16[768,768]{1,0:T(8,128)(2,1)} %bitcast.112, bf16[768,768]{1,0:T(8,128)(2,1)} %bitcast.115, bf16[768,768]{1,0:T(8,128)(2,1)} %bitcast.118, bf16[768,3072]{1,0:T(8,128)(2,1)} %bitcast.101, ...), custom_call_target="tpu_custom_call" | custom-call | tf_op jit(solution)/shard_map/front/pallas_call | solution.py:314
  22.1 6.1 %collective-permute-start = (bf16[320,768]{1,0:T(8,128)(2,1)}, bf16[320,768]{1,0:T(8,128)(2,1)S(1)}, u32[]{:S(2)}, u32[]{:S(2)}) collective-permute-start(bf16[320,768]{1,0:T(8,128)(2,1)} %front.1), channel_id=1, source_target_pairs={{0,64},{1,65},{2,66},{3,67},{4,68},{5,69},{6,70},{7,71},{8,72},{9,... | collective-permute-start | bytes 1474568 | tf_op jit(solution)/shard_map/ppermute | solution.py:930
  29.7 9.0 %collective-permute-done = bf16[320,768]{1,0:T(8,128)(2,1)S(1)} collective-permute-done((bf16[320,768]{1,0:T(8,128)(2,1)}, bf16[320,768]{1,0:T(8,128)(2,1)S(1)}, u32[]{:S(2)}, u32[]{:S(2)}) %collective-permute-start) | collective-permute-done | bytes 491552 | tf_op jit(solution)/shard_map/ppermute | solution.py:930
  39.6 32.9 %middle.1 = (f32[320,768]{1,0:T(8,128)}, bf16[320,768]{1,0:T(8,128)(2,1)}, bf16[320,3840]{1,0:T(8,128)(2,1)}, bf16[2,320,768]{2,1,0:T(8,128)(2,1)}, f32[320,768]...) custom-call(s32[4]{0:T(128)} %pad_add_fusion.3.info.refs_0_, ...), custom_call_target="tpu_custom_call" | custom-call | tf_op jit(solution)/shard_map/middle/pallas_call | solution.py:393
  75.4 14.4 %collective-permute-done.1 = bf16[320,768]{1,0:T(8,128)(2,1)S(1)} collective-permute-done((bf16[320,768]{1,0:T(8,128)(2,1)}, bf16[320,768]{1,0:T(8,128)(2,1)S(1)}, u32[]{:S(2)}, u32[]{:S(2)}) %collective-permute-start.1) | collective-permute-done | bytes 491552 | tf_op jit(solution)/shard_map/ppermute | solution.py:930
  90.7 11.7 %feed_back.1 = (f32[320,768]{1,0:T(8,128)}, bf16[320,768]{1,0:T(8,128)(2,1)}, bf16[320,768]{1,0:T(8,128)(2,1)}, f32[16,768]{1,0:T(8,128)}, bf16[320,1536]{1,0:T(8,128)(2,1)}, /*index=5*/bf16[320,2304]{1,0:T(8,128)(2,1)}) custom-call(s32[4]{0:T(128)} %pad_add_fusion.3.info.refs_0_, bf16[320,768]{1,0:T(8,128)(2,1)} %broadcast_select_fusion.upper, ...), custom_call_target="tpu_custom_call" | custom-call | tf_op jit(solution)/shard_map/feed_back/pallas_call | solution.py:469
  102.4 12.4 %attend_back.1 = (f32[256,768]{1,0:T(8,128)}, f32[38,768]{1,0:T(8,128)}, f32[16,768]{1,0:T(8,128)}, f32[12,128,128]{2,1,0:T(8,128)}, bf16[576,768]{1,0:T(8,128)(2,1)}, /*index=5*/bf16[576,768]{1,0:T(8,128)(2,1)}) custom-call(s32[4]{0:T(128)} %pad_add_fusion.3.info.refs_0_, f32[320,768]{1,0:T(8,128)} %get-tuple-element.79.total_in, ...), custom_call_target="tpu_custom_call" | custom-call | tf_op jit(solution)/shard_map/attend_back/pallas_call | solution.py:629
  114.8 1.6 copy.53
  116.6 2.0 fusion.3
  123.1 5.2 %collective-permute-done.5 = f32[4,768]{1,0:T(4,128)S(1)} collective-permute-done((f32[4,768]{1,0:T(4,128)S(1)}, f32[4,768]{1,0:T(4,128)S(1)}, u32[]{:S(2)}, u32[]{:S(2)}) %collective-permute-start.5) | collective-permute-done | bytes 12320 | tf_op jit(solution)/shard_map/ppermute | solution.py:847
  130.3 5.6 %attend_grads.1 = (bf16[224,768]{1,0:T(8,128)(2,1)}, bf16[224,768]{1,0:T(8,128)(2,1)}, bf16[224,768]{1,0:T(8,128)(2,1)}, bf16[224,768]{1,0:T(8,128)(2,1)}, bf16[...) custom-call(s32[4]{0:T(128)} %pad_add_fusion.3.info.refs_0_, ...), custom_call_target="tpu_custom_call" | custom-call | tf_op jit(solution)/shard_map/attend_grads/pallas_call | solution.py:700
  136.0 2.8 collective-permute-start.10
  139.6 4.3 %collective-permute-done.10 = bf16[224,768]{1,0:T(8,128)(2,1)S(1)} collective-permute-done((bf16[224,768]{1,0:T(8,128)(2,1)}, bf16[224,768]{1,0:T(8,128)(2,1)S(1)}, u32[]{:S(2)}, u32[]{:S(2)}) %collective-permute-start.10) | collective-permute-done | bytes 344096 | tf_op jit(solution)/shard_map/ppermute | solution.py:860
  145.0 3.7 %collective-permute-start.11 = (bf16[224,768]{1,0:T(8,128)(2,1)S(1)}, bf16[224,768]{1,0:T(8,128)(2,1)S(1)}, u32[]{:S(2)}, u32[]{:S(2)}) collective-permute-start(bf16[224,768]{1,0:T(8,128)(2,1)S(1)} %add_convert_fusion.5), channel_id=1, source_target_pairs={{0,24},{1,7},{2,26},{3,1},{4,28},{5,3},{6,30},{7,5},{8,0},{9,15},{... | collective-permute-start | bytes 1032200 | tf_op jit(solution)/shard_map/ppermute | solution.py:860
  148.8 2.0 collective-permute-start.7
  150.8 7.8 %feed_grads.1 = (bf16[384,768]{1,0:T(8,128)(2,1)}, bf16[384,768]{1,0:T(8,128)(2,1)}, bf16[384,768]{1,0:T(8,128)(2,1)}, bf16[384,768]{1,0:T(8,128)(2,1)}, bf16[38...) custom-call(s32[4]{0:T(128)} %pad_add_fusion.3.info.refs_0_, ...), custom_call_target="tpu_custom_call" | custom-call | tf_op jit(solution)/shard_map/feed_grads/pallas_call | solution.py:561
  160.4 1.6 collective-permute-start.12
  162.1 2.9 collective-permute-start.13
  168.0 5.9 %collective-permute-done.13 = bf16[112,768]{1,0:T(8,128)(2,1)S(1)} collective-permute-done((bf16[112,768]{1,0:T(8,128)(2,1)S(1)}, bf16[112,768]{1,0:T(8,128)(2,1)S(1)}, u32[]{:S(2)}, u32[]{:S(2)}) %collective-permute-start.13) | collective-permute-done | bytes 172064 | tf_op jit(solution)/shard_map/ppermute | solution.py:860
  176.7 2.6 collective-permute-done.15
  180.4 3.5 %collective-permute-done.35 = bf16[384,768]{1,0:T(8,128)(2,1)S(1)} collective-permute-done((bf16[384,768]{1,0:T(8,128)(2,1)}, bf16[384,768]{1,0:T(8,128)(2,1)S(1)}, u32[]{:S(2)}, u32[]{:S(2)}) %collective-permute-start.35) | collective-permute-done | bytes 589856 | tf_op jit(solution)/shard_map/ppermute | solution.py:860
  184.6 2.8 collective-permute-start.18
  187.4 6.3 %collective-permute-done.40 = bf16[384,768]{1,0:T(8,128)(2,1)S(1)} collective-permute-done((bf16[384,768]{1,0:T(8,128)(2,1)S(1)}, bf16[384,768]{1,0:T(8,128)(2,1)S(1)}, u32[]{:S(2)}, u32[]{:S(2)}) %collective-permute-start.40) | collective-permute-done | bytes 589856 | tf_op jit(solution)/shard_map/ppermute | solution.py:860
  193.9 3.8 %collective-permute-done.36 = bf16[384,768]{1,0:T(8,128)(2,1)S(1)} collective-permute-done((bf16[384,768]{1,0:T(8,128)(2,1)S(1)}, bf16[384,768]{1,0:T(8,128)(2,1)S(1)}, u32[]{:S(2)}, u32[]{:S(2)}) %collective-permute-start.36) | collective-permute-done | bytes 589856 | tf_op jit(solution)/shard_map/ppermute | solution.py:860
  198.1 2.7 collective-permute-start.41
  200.8 3.8 %collective-permute-start.42 = (bf16[192,768]{1,0:T(8,128)(2,1)S(1)}, bf16[192,768]{1,0:T(8,128)(2,1)S(1)}, u32[]{:S(2)}, u32[]{:S(2)}) collective-permute-start(bf16[192,768]{1,0:T(8,128)(2,1)S(1)} %get-tuple-element.169), channel_id=1, source_target_pairs={{0,4},{1,17},{2,6},{3,19},{4,0},{5,21},{6,2},{7,23},{8,12},{9,25},... | collective-permute-start | bytes 884744 | tf_op jit(solution)/shard_map/ppermute | solution.py:860
  204.6 2.5 collective-permute-start.43
  207.2 5.2 %collective-permute-done.42 = bf16[192,768]{1,0:T(8,128)(2,1)S(1)} collective-permute-done((bf16[192,768]{1,0:T(8,128)(2,1)S(1)}, bf16[192,768]{1,0:T(8,128)(2,1)S(1)}, u32[]{:S(2)}, u32[]{:S(2)}) %collective-permute-start.42) | collective-permute-done | bytes 294944 | tf_op jit(solution)/shard_map/ppermute | solution.py:860
  213.6 4.1 %collective-permute-done.44 = bf16[96,768]{1,0:T(8,128)(2,1)S(1)} collective-permute-done((bf16[96,768]{1,0:T(8,128)(2,1)S(1)}, bf16[96,768]{1,0:T(8,128)(2,1)S(1)}, u32[]{:S(2)}, u32[]{:S(2)}) %collective-permute-start.44) | collective-permute-done | bytes 147488 | tf_op jit(solution)/shard_map/ppermute | solution.py:847
  219.1 3.2 %collective-permute-start.22 = (bf16[224,768]{1,0:T(8,128)(2,1)S(1)}, bf16[224,768]{1,0:T(8,128)(2,1)S(1)}, u32[]{:S(2)}, u32[]{:S(2)}) collective-permute-start(bf16[224,768]{1,0:T(8,128)(2,1)S(1)} %bitcast.148), channel_id=1, source_target_pairs={{0,24},{1,7},{2,26},{3,1},{4,28},{5,3},{6,30},{7,5},{8,0},{9,15},{... | collective-permute-start | bytes 1032200 | tf_op jit(solution)/shard_map/ppermute | solution.py:860
  223.1 2.8 collective-permute-start.46
  227.7 2.5 collective-permute-start.27
  230.2 3.3 %collective-permute-done.22.refs_4_ = bf16[224,768]{1,0:T(8,128)(2,1)S(1)} collective-permute-done((bf16[224,768]{1,0:T(8,128)(2,1)S(1)}, bf16[224,768]{1,0:T(8,128)(2,1)S(1)}, u32[]{:S(2)}, u32[]{:S(2)}) %collective-permute-start.22) | collective-permute-done | bytes 344096 | tf_op jit(solution)/shard_map/ppermute | solution.py:860
  234.4 2.1 collective-permute-start.48
  237.1 3.8 %collective-permute-start.23 = (bf16[224,768]{1,0:T(8,128)(2,1)S(1)}, bf16[224,768]{1,0:T(8,128)(2,1)S(1)}, u32[]{:S(2)}, u32[]{:S(2)}) collective-permute-start(bf16[224,768]{1,0:T(8,128)(2,1)S(1)} %collective-permute-done.22.refs_4_), channel_id=1, source_target_pairs={{0,24},{1,7},{2,26},{3,1},{4,28},{5,3},{6,30},{7,5},{8,0},{9,15},{... | collective-permute-start | bytes 1032200 | tf_op jit(solution)/shard_map/ppermute | solution.py:860
  241.0 4.5 %collective-permute-done.48 = bf16[192,768]{1,0:T(8,128)(2,1)S(1)} collective-permute-done((bf16[192,768]{1,0:T(8,128)(2,1)S(1)}, bf16[192,768]{1,0:T(8,128)(2,1)S(1)}, u32[]{:S(2)}, u32[]{:S(2)}) %collective-permute-start.48) | collective-permute-done | bytes 294944 | tf_op jit(solution)/shard_map/ppermute | solution.py:860
  246.5 3.2 %collective-permute-start.51 = (bf16[384,768]{1,0:T(8,128)(2,1)S(1)}, bf16[384,768]{1,0:T(8,128)(2,1)S(1)}, u32[]{:S(2)}, u32[]{:S(2)}) collective-permute-start(bf16[384,768]{1,0:T(8,128)(2,1)S(1)} %bitcast.131), channel_id=1, source_target_pairs={{0,24},{1,7},{2,26},{3,1},{4,28},{5,3},{6,30},{7,5},{8,0},{9,15},{... | collective-permute-start | bytes 1769480 | tf_op jit(solution)/shard_map/ppermute | solution.py:860
  249.7 3.2 %collective-permute-start.56 = (bf16[384,768]{1,0:T(8,128)(2,1)S(1)}, bf16[384,768]{1,0:T(8,128)(2,1)S(1)}, u32[]{:S(2)}, u32[]{:S(2)}) collective-permute-start(bf16[384,768]{1,0:T(8,128)(2,1)S(1)} %bitcast.136), channel_id=1, source_target_pairs={{0,24},{1,7},{2,26},{3,1},{4,28},{5,3},{6,30},{7,5},{8,0},{9,15},{... | collective-permute-start | bytes 1769480 | tf_op jit(solution)/shard_map/ppermute | solution.py:860
  252.9 1.6 collective-permute-done.25.refs_4_
  254.7 2.8 collective-permute-done.49.refs_3_
  258.3 5.6 %collective-permute-done.55.refs_5_ = bf16[384,768]{1,0:T(8,128)(2,1)S(1)} collective-permute-done((bf16[384,768]{1,0:T(8,128)(2,1)S(1)}, bf16[384,768]{1,0:T(8,128)(2,1)S(1)}, u32[]{:S(2)}, u32[]{:S(2)}) %collective-permute-start.55) | collective-permute-done | bytes 589856 | tf_op jit(solution)/shard_map/ppermute | solution.py:860
  264.1 3.2 %collective-permute-start.52 = (bf16[384,768]{1,0:T(8,128)(2,1)S(1)}, bf16[384,768]{1,0:T(8,128)(2,1)}, u32[]{:S(2)}, u32[]{:S(2)}) collective-permute-start(bf16[384,768]{1,0:T(8,128)(2,1)S(1)} %collective-permute-done.51.refs_4_), channel_id=1, source_target_pairs={{0,24},{1,7},{2,26},{3,1},{4,28},{5,3},{6,30},{7,5},{8,0},{9,15},{... | collective-permute-start | bytes 1769480 | tf_op jit(solution)/shard_map/ppermute | solution.py:860
  268.7 6.6 %collective-permute-done.50.refs_1_ = bf16[384,768]{1,0:T(8,128)(2,1)} collective-permute-done((bf16[384,768]{1,0:T(8,128)(2,1)S(1)}, bf16[384,768]{1,0:T(8,128)(2,1)}, u32[]{:S(2)}, u32[]{:S(2)}) %collective-permute-start.50) | collective-permute-done | bytes 589856 | tf_op jit(solution)/shard_map/ppermute | solution.py:860
  281.4 4.9 %attend_out_a.1 = (f32[768,768]{1,0:T(8,128)}, f32[768,768]{1,0:T(8,128)}, f32[768,768]{1,0:T(8,128)}, f32[768,768]{1,0:T(8,128)}) custom-call(s32[4]{0:T(128)} %pad_add_fusion.3.info.refs_0_, bf16[224,768]{1,0:T(8,128)(2,1)} %bitcast.147, bf16[224,768]{1,0:T(8,128)(2,1)} %bitcast.151, bf16[224,768]{1,0:T(8,128)(2,1)} %copy-done.28, ...), custom_call_target="tpu_custom_call" | custom-call | bytes 12386304 | tf_op jit(solution)/shard_map/attend_out_a/pallas_call | solution.py:784
  286.4 3.2 %attend_out_b.1 = (f32[768,768]{1,0:T(8,128)}, f32[768,768]{1,0:T(8,128)}, f32[768,768]{1,0:T(8,128)}, f32[768,768]{1,0:T(8,128)}) custom-call(s32[4]{0:T(128)} %pad_add_fusion.3.info.refs_0_, bf16[224,768]{1,0:T(8,128)(2,1)} %copy-done.21, bf16[224,768]{1,0:T(8,128)(2,1)} %copy-done.22, ...), custom_call_target="tpu_custom_call", output_to_operand_aliasing={{0}: (5, {}), {1}: (6, {}), {2}: (7, {}), {3}: (8, {})} | custom-call | bytes 4128768 | tf_op jit(solution)/shard_map/attend_out_b/pallas_call | solution.py:784
  289.6 7.7 %feed_out_a.1 = (f32[3072,768]{1,0:T(8,128)}, f32[768,3072]{1,0:T(8,128)}) custom-call(s32[4]{0:T(128)} %pad_add_fusion.3.info.refs_0_, bf16[384,768]{1,0:T(8,128)(2,1)} %bitcast.138, bf16[384,768]{1,0:T(8,128)(2,1)} %bitcast.134, bf16[384,768]{1,0:T(8,128)(2,1)} %copy-done.9, bf16[384,768]{1,0:T(8,128)(2,1)} %copy-done.10, bf16[384,768]{1,0:T(8,128)(2,1)} %copy-done.11, ...), custom_call_target="tpu_custom_call" | custom-call | bytes 21233664 | tf_op jit(solution)/shard_map/feed_out_a/pallas_call | solution.py:784
  297.3 4.2 %feed_out_b.1 = (f32[3072,768]{1,0:T(8,128)}, f32[768,3072]{1,0:T(8,128)}) custom-call(s32[4]{0:T(128)} %pad_add_fusion.3.info.refs_0_, bf16[384,768]{1,0:T(8,128)(2,1)} %collective-permute-done.50.refs_1_, bf16[384,768]{1,0:T(8,128)(2,1)} %collective-permute-done.52.refs_2_, ...), custom_call_target="tpu_custom_call", output_to_operand_aliasing={{0}: (5, {}), {1}: (6, {})} | custom-call | bytes 7077888 | tf_op jit(solution)/shard_map/feed_out_b/pallas_call | solution.py:784
  (268 shorter events, 48.9 us)
Async XLA Ops:
  22.1 16.6 %collective-permute-start = (bf16[320,768]{1,0:T(8,128)(2,1)}, bf16[320,768]{1,0:T(8,128)(2,1)S(1)}, u32[]{:S(2)}, u32[]{:S(2)}) collective-permute-start(bf16[320,768]{1,0:T(8,128)(2,1)} %front.1), channel_id=1, source_target_pairs={{0,64},{1,65},{2,66},{3,67},{4,68},{5,69},{6,70},{7,71},{8,72},{9,... | collective-permute-start | bytes 1474568 | tf_op jit(solution)/shard_map/ppermute | solution.py:930
  72.5 56.4 %collective-permute-start.2 = (bf16[320,3840]{1,0:T(8,128)(2,1)}, bf16[320,3840]{1,0:T(8,128)(2,1)S(1)}, u32[]{:S(2)}, u32[]{:S(2)}) collective-permute-start(bf16[320,3840]{1,0:T(8,128)(2,1)} %get-tuple-element.90), channel_id=1, source_target_pairs={{0,1},{1,0},{2,3},{3,2},{4,5},{5,4},{6,7},{7,6},{8,9},{9,8},{10,11... | collective-permute-start | bytes 7372808 | tf_op jit(solution)/shard_map/ppermute | solution.py:847
  72.6 17.2 %collective-permute-start.1 = (bf16[320,768]{1,0:T(8,128)(2,1)}, bf16[320,768]{1,0:T(8,128)(2,1)S(1)}, u32[]{:S(2)}, u32[]{:S(2)}) collective-permute-start(bf16[320,768]{1,0:T(8,128)(2,1)} %get-tuple-element.73), channel_id=1, source_target_pairs={{64,0},{65,1},{66,2},{67,3},{68,4},{69,5},{70,6},{71,7},{72,8},{73... | collective-permute-start | bytes 1474568 | tf_op jit(solution)/shard_map/ppermute | solution.py:930
  116.5 12.4 %collective-permute-start.3 = (bf16[576,768]{1,0:T(8,128)(2,1)}, bf16[576,768]{1,0:T(8,128)(2,1)}, u32[]{:S(2)}, u32[]{:S(2)}) collective-permute-start(bf16[576,768]{1,0:T(8,128)(2,1)} %get-tuple-element.92), channel_id=1, source_target_pairs={{0,1},{1,0},{2,3},{3,2},{4,5},{5,4},{6,7},{7,6},{8,9},{9,8},{10,11... | collective-permute-start | bytes 2654216 | tf_op jit(solution)/shard_map/ppermute | solution.py:847
  120.8 30.0 %collective-permute-start.34 = (bf16[320,2304]{1,0:T(8,128)(2,1)}, bf16[320,2304]{1,0:T(8,128)(2,1)}, u32[]{:S(2)}, u32[]{:S(2)}) collective-permute-start(bf16[320,2304]{1,0:T(8,128)(2,1)} %get-tuple-element.115), channel_id=1, source_target_pairs={{0,1},{1,0},{2,3},{3,2},{4,5},{5,4},{6,7},{7,6},{8,9},{9,8},{10,11... | collective-permute-start | bytes 4423688 | tf_op jit(solution)/shard_map/ppermute | solution.py:847
  136.0 7.9 %collective-permute-start.10 = (bf16[224,768]{1,0:T(8,128)(2,1)}, bf16[224,768]{1,0:T(8,128)(2,1)S(1)}, u32[]{:S(2)}, u32[]{:S(2)}) collective-permute-start(bf16[224,768]{1,0:T(8,128)(2,1)} %get-tuple-element.102), channel_id=1, source_target_pairs={{0,24},{1,7},{2,26},{3,1},{4,28},{5,3},{6,30},{7,5},{8,0},{9,15},{... | collective-permute-start | bytes 1032200 | tf_op jit(solution)/shard_map/ppermute | solution.py:860
  138.8 9.9 %collective-permute-start.6 = (bf16[224,768]{1,0:T(8,128)(2,1)}, bf16[224,768]{1,0:T(8,128)(2,1)S(1)}, u32[]{:S(2)}, u32[]{:S(2)}) collective-permute-start(bf16[224,768]{1,0:T(8,128)(2,1)} %get-tuple-element.97), channel_id=1, source_target_pairs={{0,8},{1,3},{2,10},{3,5},{4,12},{5,7},{6,14},{7,1},{8,16},{9,11},{... | collective-permute-start | bytes 1032200 | tf_op jit(solution)/shard_map/ppermute | solution.py:860
  138.8 21.2 %collective-permute-start.9 = (bf16[224,768]{1,0:T(8,128)(2,1)}, bf16[224,768]{1,0:T(8,128)(2,1)S(1)}, u32[]{:S(2)}, u32[]{:S(2)}) collective-permute-start(bf16[224,768]{1,0:T(8,128)(2,1)} %get-tuple-element.100), channel_id=1, source_target_pairs={{0,8},{1,3},{2,10},{3,5},{4,12},{5,7},{6,14},{7,1},{8,16},{9,11},{... | collective-permute-start | bytes 1032200 | tf_op jit(solution)/shard_map/ppermute | solution.py:860
  145.0 15.1 %collective-permute-start.11 = (bf16[224,768]{1,0:T(8,128)(2,1)S(1)}, bf16[224,768]{1,0:T(8,128)(2,1)S(1)}, u32[]{:S(2)}, u32[]{:S(2)}) collective-permute-start(bf16[224,768]{1,0:T(8,128)(2,1)S(1)} %add_convert_fusion.5), channel_id=1, source_target_pairs={{0,24},{1,7},{2,26},{3,1},{4,28},{5,3},{6,30},{7,5},{8,0},{9,15},{... | collective-permute-start | bytes 1032200 | tf_op jit(solution)/shard_map/ppermute | solution.py:860
  148.6 11.6 %collective-permute-start.8 = (bf16[224,768]{1,0:T(8,128)(2,1)}, bf16[224,768]{1,0:T(8,128)(2,1)S(1)}, u32[]{:S(2)}, u32[]{:S(2)}) collective-permute-start(bf16[224,768]{1,0:T(8,128)(2,1)} %get-tuple-element.98), channel_id=1, source_target_pairs={{0,24},{1,7},{2,26},{3,1},{4,28},{5,3},{6,30},{7,5},{8,0},{9,15},{... | collective-permute-start | bytes 1032200 | tf_op jit(solution)/shard_map/ppermute | solution.py:860
  148.8 11.4 %collective-permute-start.7 = (bf16[224,768]{1,0:T(8,128)(2,1)S(1)}, bf16[224,768]{1,0:T(8,128)(2,1)S(1)}, u32[]{:S(2)}, u32[]{:S(2)}) collective-permute-start(bf16[224,768]{1,0:T(8,128)(2,1)S(1)} %add_convert_fusion.7), channel_id=1, source_target_pairs={{0,8},{1,3},{2,10},{3,5},{4,12},{5,7},{6,14},{7,1},{8,16},{9,11},{... | collective-permute-start | bytes 1032200 | tf_op jit(solution)/shard_map/ppermute | solution.py:860
  158.7 17.1 %collective-permute-start.39 = (bf16[384,768]{1,0:T(8,128)(2,1)}, bf16[384,768]{1,0:T(8,128)(2,1)S(1)}, u32[]{:S(2)}, u32[]{:S(2)}) collective-permute-start(bf16[384,768]{1,0:T(8,128)(2,1)} %get-tuple-element.123), channel_id=1, source_target_pairs={{0,24},{1,7},{2,26},{3,1},{4,28},{5,3},{6,30},{7,5},{8,0},{9,15},{... | collective-permute-start | bytes 1769480 | tf_op jit(solution)/shard_map/ppermute | solution.py:860
  162.1 11.7 %collective-permute-start.13 = (bf16[112,768]{1,0:T(8,128)(2,1)S(1)}, bf16[112,768]{1,0:T(8,128)(2,1)S(1)}, u32[]{:S(2)}, u32[]{:S(2)}) collective-permute-start(bf16[112,768]{1,0:T(8,128)(2,1)S(1)} %get-tuple-element.176), channel_id=1, source_target_pairs={{0,4},{1,17},{2,6},{3,19},{4,0},{5,21},{6,2},{7,23},{8,12},{9,25},... | collective-permute-start | bytes 516104 | tf_op jit(solution)/shard_map/ppermute | solution.py:860
  165.0 9.6 %collective-permute-start.14 = (bf16[112,768]{1,0:T(8,128)(2,1)S(1)}, bf16[112,768]{1,0:T(8,128)(2,1)S(1)}, u32[]{:S(2)}, u32[]{:S(2)}) collective-permute-start(bf16[112,768]{1,0:T(8,128)(2,1)S(1)} %get-tuple-element.177), channel_id=1, source_target_pairs={{0,6},{1,25},{2,0},{3,27},{4,2},{5,29},{6,4},{7,31},{8,14},{9,1},{... | collective-permute-start | bytes 516104 | tf_op jit(solution)/shard_map/ppermute | solution.py:860
  166.3 18.3 %collective-permute-start.38 = (bf16[384,768]{1,0:T(8,128)(2,1)}, bf16[384,768]{1,0:T(8,128)(2,1)S(1)}, u32[]{:S(2)}, u32[]{:S(2)}) collective-permute-start(bf16[384,768]{1,0:T(8,128)(2,1)} %get-tuple-element.121), channel_id=1, source_target_pairs={{0,8},{1,3},{2,10},{3,5},{4,12},{5,7},{6,14},{7,1},{8,16},{9,11},{... | collective-permute-start | bytes 1769480 | tf_op jit(solution)/shard_map/ppermute | solution.py:860
  167.4 16.6 %collective-permute-start.35 = (bf16[384,768]{1,0:T(8,128)(2,1)}, bf16[384,768]{1,0:T(8,128)(2,1)S(1)}, u32[]{:S(2)}, u32[]{:S(2)}) collective-permute-start(bf16[384,768]{1,0:T(8,128)(2,1)} %get-tuple-element.118), channel_id=1, source_target_pairs={{0,8},{1,3},{2,10},{3,5},{4,12},{5,7},{6,14},{7,1},{8,16},{9,11},{... | collective-permute-start | bytes 1769480 | tf_op jit(solution)/shard_map/ppermute | solution.py:860
  173.8 20.1 %collective-permute-start.37 = (bf16[384,768]{1,0:T(8,128)(2,1)S(1)}, bf16[384,768]{1,0:T(8,128)(2,1)S(1)}, u32[]{:S(2)}, u32[]{:S(2)}) collective-permute-start(bf16[384,768]{1,0:T(8,128)(2,1)S(1)} %copy-done.50), channel_id=1, source_target_pairs={{0,24},{1,7},{2,26},{3,1},{4,28},{5,3},{6,30},{7,5},{8,0},{9,15},{... | collective-permute-start | bytes 1769480 | tf_op jit(solution)/shard_map/ppermute | solution.py:860
  176.0 17.7 %collective-permute-start.40 = (bf16[384,768]{1,0:T(8,128)(2,1)S(1)}, bf16[384,768]{1,0:T(8,128)(2,1)S(1)}, u32[]{:S(2)}, u32[]{:S(2)}) collective-permute-start(bf16[384,768]{1,0:T(8,128)(2,1)S(1)} %add_convert_fusion.1), channel_id=1, source_target_pairs={{0,24},{1,7},{2,26},{3,1},{4,28},{5,3},{6,30},{7,5},{8,0},{9,15},{... | collective-permute-start | bytes 1769480 | tf_op jit(solution)/shard_map/ppermute | solution.py:860
  184.1 13.7 %collective-permute-start.36 = (bf16[384,768]{1,0:T(8,128)(2,1)S(1)}, bf16[384,768]{1,0:T(8,128)(2,1)S(1)}, u32[]{:S(2)}, u32[]{:S(2)}) collective-permute-start(bf16[384,768]{1,0:T(8,128)(2,1)S(1)} %add_convert_fusion.3), channel_id=1, source_target_pairs={{0,8},{1,3},{2,10},{3,5},{4,12},{5,7},{6,14},{7,1},{8,16},{9,11},{... | collective-permute-start | bytes 1769480 | tf_op jit(solution)/shard_map/ppermute | solution.py:860
  184.4 20.1 %collective-permute-start.17 = (bf16[112,768]{1,0:T(8,128)(2,1)S(1)}, bf16[112,768]{1,0:T(8,128)(2,1)S(1)}, u32[]{:S(2)}, u32[]{:S(2)}) collective-permute-start(bf16[112,768]{1,0:T(8,128)(2,1)S(1)} %pad_maximum_fusion.3), channel_id=1, source_target_pairs={{0,6},{1,25},{2,0},{3,27},{4,2},{5,29},{6,4},{7,31},{8,14},{9,1},{... | collective-permute-start | bytes 516104 | tf_op jit(solution)/shard_map/ppermute | solution.py:860
  184.6 22.5 %collective-permute-start.18 = (bf16[112,768]{1,0:T(8,128)(2,1)S(1)}, bf16[112,768]{1,0:T(8,128)(2,1)S(1)}, u32[]{:S(2)}, u32[]{:S(2)}) collective-permute-start(bf16[112,768]{1,0:T(8,128)(2,1)S(1)} %pad_maximum_fusion.3), channel_id=1, source_target_pairs={{0,4},{1,17},{2,6},{3,19},{4,0},{5,21},{6,2},{7,23},{8,12},{9,25},... | collective-permute-start | bytes 516104 | tf_op jit(solution)/shard_map/ppermute | solution.py:860
  193.7 19.9 %collective-permute-start.19 = (bf16[112,768]{1,0:T(8,128)(2,1)S(1)}, bf16[112,768]{1,0:T(8,128)(2,1)S(1)}, u32[]{:S(2)}, u32[]{:S(2)}) collective-permute-start(bf16[112,768]{1,0:T(8,128)(2,1)S(1)} %pad_maximum_fusion.3), channel_id=1, source_target_pairs={{0,2},{1,9},{2,4},{3,11},{4,6},{5,13},{6,0},{7,15},{8,10},{9,17},{... | collective-permute-start | bytes 516104 | tf_op jit(solution)/shard_map/ppermute | solution.py:860
  198.1 9.1 %collective-permute-start.41 = (bf16[192,768]{1,0:T(8,128)(2,1)S(1)}, bf16[192,768]{1,0:T(8,128)(2,1)S(1)}, u32[]{:S(2)}, u32[]{:S(2)}) collective-permute-start(bf16[192,768]{1,0:T(8,128)(2,1)S(1)} %get-tuple-element.168), channel_id=1, source_target_pairs={{0,2},{1,9},{2,4},{3,11},{4,6},{5,13},{6,0},{7,15},{8,10},{9,17},{... | collective-permute-start | bytes 884744 | tf_op jit(solution)/shard_map/ppermute | solution.py:860
  200.8 11.5 %collective-permute-start.42 = (bf16[192,768]{1,0:T(8,128)(2,1)S(1)}, bf16[192,768]{1,0:T(8,128)(2,1)S(1)}, u32[]{:S(2)}, u32[]{:S(2)}) collective-permute-start(bf16[192,768]{1,0:T(8,128)(2,1)S(1)} %get-tuple-element.169), channel_id=1, source_target_pairs={{0,4},{1,17},{2,6},{3,19},{4,0},{5,21},{6,2},{7,23},{8,12},{9,25},... | collective-permute-start | bytes 884744 | tf_op jit(solution)/shard_map/ppermute | solution.py:860
  219.0 8.6 %collective-permute-start.20 = (bf16[224,768]{1,0:T(8,128)(2,1)S(1)}, bf16[224,768]{1,0:T(8,128)(2,1)S(1)}, u32[]{:S(2)}, u32[]{:S(2)}) collective-permute-start(bf16[224,768]{1,0:T(8,128)(2,1)S(1)} %bitcast.144), channel_id=1, source_target_pairs={{0,8},{1,3},{2,10},{3,5},{4,12},{5,7},{6,14},{7,1},{8,16},{9,11},{... | collective-permute-start | bytes 1032200 | tf_op jit(solution)/shard_map/ppermute | solution.py:860
  219.1 14.3 %collective-permute-start.22 = (bf16[224,768]{1,0:T(8,128)(2,1)S(1)}, bf16[224,768]{1,0:T(8,128)(2,1)S(1)}, u32[]{:S(2)}, u32[]{:S(2)}) collective-permute-start(bf16[224,768]{1,0:T(8,128)(2,1)S(1)} %bitcast.148), channel_id=1, source_target_pairs={{0,24},{1,7},{2,26},{3,1},{4,28},{5,3},{6,30},{7,5},{8,0},{9,15},{... | collective-permute-start | bytes 1032200 | tf_op jit(solution)/shard_map/ppermute | solution.py:860
  222.3 12.1 %collective-permute-start.26 = (bf16[224,768]{1,0:T(8,128)(2,1)S(1)}, bf16[224,768]{1,0:T(8,128)(2,1)S(1)}, u32[]{:S(2)}, u32[]{:S(2)}) collective-permute-start(bf16[224,768]{1,0:T(8,128)(2,1)S(1)} %bitcast.149), channel_id=1, source_target_pairs={{0,8},{1,3},{2,10},{3,5},{4,12},{5,7},{6,14},{7,1},{8,16},{9,11},{... | collective-permute-start | bytes 1032200 | tf_op jit(solution)/shard_map/ppermute | solution.py:860
  223.1 11.3 %collective-permute-start.46 = (bf16[192,768]{1,0:T(8,128)(2,1)S(1)}, bf16[192,768]{1,0:T(8,128)(2,1)S(1)}, u32[]{:S(2)}, u32[]{:S(2)}) collective-permute-start(bf16[192,768]{1,0:T(8,128)(2,1)S(1)} %pad_maximum_fusion.2), channel_id=1, source_target_pairs={{0,6},{1,25},{2,0},{3,27},{4,2},{5,29},{6,4},{7,31},{8,14},{9,1},{... | collective-permute-start | bytes 884744 | tf_op jit(solution)/shard_map/ppermute | solution.py:860
  225.9 10.7 %collective-permute-start.47 = (bf16[192,768]{1,0:T(8,128)(2,1)S(1)}, bf16[192,768]{1,0:T(8,128)(2,1)S(1)}, u32[]{:S(2)}, u32[]{:S(2)}) collective-permute-start(bf16[192,768]{1,0:T(8,128)(2,1)S(1)} %pad_maximum_fusion.2), channel_id=1, source_target_pairs={{0,4},{1,17},{2,6},{3,19},{4,0},{5,21},{6,2},{7,23},{8,12},{9,25},... | collective-permute-start | bytes 884744 | tf_op jit(solution)/shard_map/ppermute | solution.py:860
  227.7 9.5 %collective-permute-start.27 = (bf16[224,768]{1,0:T(8,128)(2,1)S(1)}, bf16[224,768]{1,0:T(8,128)(2,1)S(1)}, u32[]{:S(2)}, u32[]{:S(2)}) collective-permute-start(bf16[224,768]{1,0:T(8,128)(2,1)S(1)} %bitcast.145), channel_id=1, source_target_pairs={{0,24},{1,7},{2,26},{3,1},{4,28},{5,3},{6,30},{7,5},{8,0},{9,15},{... | collective-permute-start | bytes 1032200 | tf_op jit(solution)/shard_map/ppermute | solution.py:860
  234.4 11.1 %collective-permute-start.48 = (bf16[192,768]{1,0:T(8,128)(2,1)S(1)}, bf16[192,768]{1,0:T(8,128)(2,1)S(1)}, u32[]{:S(2)}, u32[]{:S(2)}) collective-permute-start(bf16[192,768]{1,0:T(8,128)(2,1)S(1)} %pad_maximum_fusion.2), channel_id=1, source_target_pairs={{0,2},{1,9},{2,4},{3,11},{4,6},{5,13},{6,0},{7,15},{8,10},{9,17},{... | collective-permute-start | bytes 884744 | tf_op jit(solution)/shard_map/ppermute | solution.py:860
  236.5 9.1 %collective-permute-start.21 = (bf16[224,768]{1,0:T(8,128)(2,1)S(1)}, bf16[224,768]{1,0:T(8,128)(2,1)S(1)}, u32[]{:S(2)}, u32[]{:S(2)}) collective-permute-start(bf16[224,768]{1,0:T(8,128)(2,1)S(1)} %collective-permute-done.20.refs_3_), channel_id=1, source_target_pairs={{0,8},{1,3},{2,10},{3,5},{4,12},{5,7},{6,14},{7,1},{8,16},{9,11},{... | collective-permute-start | bytes 1032200 | tf_op jit(solution)/shard_map/ppermute | solution.py:860
  237.1 9.2 %collective-permute-start.31 = (bf16[224,768]{1,0:T(8,128)(2,1)S(1)}, bf16[224,768]{1,0:T(8,128)(2,1)S(1)}, u32[]{:S(2)}, u32[]{:S(2)}) collective-permute-start(bf16[224,768]{1,0:T(8,128)(2,1)S(1)} %collective-permute-done.22.refs_4_), channel_id=1, source_target_pairs={{0,1},{1,0},{2,3},{3,2},{4,5},{5,4},{6,7},{7,6},{8,9},{9,8},{10,11... | collective-permute-start | bytes 1032200 | tf_op jit(solution)/shard_map/ppermute | solution.py:847
  237.1 12.5 %collective-permute-start.23 = (bf16[224,768]{1,0:T(8,128)(2,1)S(1)}, bf16[224,768]{1,0:T(8,128)(2,1)S(1)}, u32[]{:S(2)}, u32[]{:S(2)}) collective-permute-start(bf16[224,768]{1,0:T(8,128)(2,1)S(1)} %collective-permute-done.22.refs_4_), channel_id=1, source_target_pairs={{0,24},{1,7},{2,26},{3,1},{4,28},{5,3},{6,30},{7,5},{8,0},{9,15},{... | collective-permute-start | bytes 1032200 | tf_op jit(solution)/shard_map/ppermute | solution.py:860
  246.3 11.2 %collective-permute-start.49 = (bf16[384,768]{1,0:T(8,128)(2,1)S(1)}, bf16[384,768]{1,0:T(8,128)(2,1)S(1)}, u32[]{:S(2)}, u32[]{:S(2)}) collective-permute-start(bf16[384,768]{1,0:T(8,128)(2,1)S(1)} %bitcast.135), channel_id=1, source_target_pairs={{0,8},{1,3},{2,10},{3,5},{4,12},{5,7},{6,14},{7,1},{8,16},{9,11},{... | collective-permute-start | bytes 1769480 | tf_op jit(solution)/shard_map/ppermute | solution.py:860
  246.5 11.1 %collective-permute-start.51 = (bf16[384,768]{1,0:T(8,128)(2,1)S(1)}, bf16[384,768]{1,0:T(8,128)(2,1)S(1)}, u32[]{:S(2)}, u32[]{:S(2)}) collective-permute-start(bf16[384,768]{1,0:T(8,128)(2,1)S(1)} %bitcast.131), channel_id=1, source_target_pairs={{0,24},{1,7},{2,26},{3,1},{4,28},{5,3},{6,30},{7,5},{8,0},{9,15},{... | collective-permute-start | bytes 1769480 | tf_op jit(solution)/shard_map/ppermute | solution.py:860
  249.7 14.2 %collective-permute-start.55 = (bf16[384,768]{1,0:T(8,128)(2,1)S(1)}, bf16[384,768]{1,0:T(8,128)(2,1)S(1)}, u32[]{:S(2)}, u32[]{:S(2)}) collective-permute-start(bf16[384,768]{1,0:T(8,128)(2,1)S(1)} %bitcast.132), channel_id=1, source_target_pairs={{0,8},{1,3},{2,10},{3,5},{4,12},{5,7},{6,14},{7,1},{8,16},{9,11},{... | collective-permute-start | bytes 1769480 | tf_op jit(solution)/shard_map/ppermute | solution.py:860
  249.7 14.4 %collective-permute-start.56 = (bf16[384,768]{1,0:T(8,128)(2,1)S(1)}, bf16[384,768]{1,0:T(8,128)(2,1)S(1)}, u32[]{:S(2)}, u32[]{:S(2)}) collective-permute-start(bf16[384,768]{1,0:T(8,128)(2,1)S(1)} %bitcast.136), channel_id=1, source_target_pairs={{0,24},{1,7},{2,26},{3,1},{4,28},{5,3},{6,30},{7,5},{8,0},{9,15},{... | collective-permute-start | bytes 1769480 | tf_op jit(solution)/shard_map/ppermute | solution.py:860
  254.6 13.5 %collective-permute-start.57 = (bf16[384,768]{1,0:T(8,128)(2,1)S(1)}, bf16[384,768]{1,0:T(8,128)(2,1)S(1)}, u32[]{:S(2)}, u32[]{:S(2)}) collective-permute-start(bf16[384,768]{1,0:T(8,128)(2,1)S(1)} %bitcast.137), channel_id=1, source_target_pairs={{0,1},{1,0},{2,3},{3,2},{4,5},{5,4},{6,7},{7,6},{8,9},{9,8},{10,11... | collective-permute-start | bytes 1769480 | tf_op jit(solution)/shard_map/ppermute | solution.py:847
  257.5 10.5 %collective-permute-start.58 = (bf16[384,768]{1,0:T(8,128)(2,1)S(1)}, bf16[384,768]{1,0:T(8,128)(2,1)S(1)}, u32[]{:S(2)}, u32[]{:S(2)}) collective-permute-start(bf16[384,768]{1,0:T(8,128)(2,1)S(1)} %bitcast.133), channel_id=1, source_target_pairs={{0,1},{1,0},{2,3},{3,2},{4,5},{5,4},{6,7},{7,6},{8,9},{9,8},{10,11... | collective-permute-start | bytes 1769480 | tf_op jit(solution)/shard_map/ppermute | solution.py:847
  257.5 11.0 %collective-permute-start.59 = (bf16[384,768]{1,0:T(8,128)(2,1)S(1)}, bf16[384,768]{1,0:T(8,128)(2,1)S(1)}, u32[]{:S(2)}, u32[]{:S(2)}) collective-permute-start(bf16[384,768]{1,0:T(8,128)(2,1)S(1)} %collective-permute-done.49.refs_3_), channel_id=1, source_target_pairs={{0,1},{1,0},{2,3},{3,2},{4,5},{5,4},{6,7},{7,6},{8,9},{9,8},{10,11... | collective-permute-start | bytes 1769480 | tf_op jit(solution)/shard_map/ppermute | solution.py:847
  263.8 11.4 %collective-permute-start.50 = (bf16[384,768]{1,0:T(8,128)(2,1)S(1)}, bf16[384,768]{1,0:T(8,128)(2,1)}, u32[]{:S(2)}, u32[]{:S(2)}) collective-permute-start(bf16[384,768]{1,0:T(8,128)(2,1)S(1)} %collective-permute-done.49.refs_3_), channel_id=1, source_target_pairs={{0,8},{1,3},{2,10},{3,5},{4,12},{5,7},{6,14},{7,1},{8,16},{9,11},{... | collective-permute-start | bytes 1769480 | tf_op jit(solution)/shard_map/ppermute | solution.py:860
  264.1 11.2 %collective-permute-start.52 = (bf16[384,768]{1,0:T(8,128)(2,1)S(1)}, bf16[384,768]{1,0:T(8,128)(2,1)}, u32[]{:S(2)}, u32[]{:S(2)}) collective-permute-start(bf16[384,768]{1,0:T(8,128)(2,1)S(1)} %collective-permute-done.51.refs_4_), channel_id=1, source_target_pairs={{0,24},{1,7},{2,26},{3,1},{4,28},{5,3},{6,30},{7,5},{8,0},{9,15},{... | collective-permute-start | bytes 1769480 | tf_op jit(solution)/shard_map/ppermute | solution.py:860
  268.0 21.5 %collective-permute-start.60 = (bf16[384,768]{1,0:T(8,128)(2,1)S(1)}, bf16[384,768]{1,0:T(8,128)(2,1)}, u32[]{:S(2)}, u32[]{:S(2)}) collective-permute-start(bf16[384,768]{1,0:T(8,128)(2,1)S(1)} %collective-permute-done.51.refs_4_), channel_id=1, source_target_pairs={{0,1},{1,0},{2,3},{3,2},{4,5},{5,4},{6,7},{7,6},{8,9},{9,8},{10,11... | collective-permute-start | bytes 1769480 | tf_op jit(solution)/shard_map/ppermute | solution.py:847
  268.1 21.5 %collective-permute-start.61 = (bf16[384,768]{1,0:T(8,128)(2,1)S(1)}, bf16[384,768]{1,0:T(8,128)(2,1)}, u32[]{:S(2)}, u32[]{:S(2)}) collective-permute-start(bf16[384,768]{1,0:T(8,128)(2,1)S(1)} %collective-permute-done.55.refs_5_), channel_id=1, source_target_pairs={{0,1},{1,0},{2,3},{3,2},{4,5},{5,4},{6,7},{7,6},{8,9},{9,8},{10,11... | collective-permute-start | bytes 1769480 | tf_op jit(solution)/shard_map/ppermute | solution.py:847
  268.6 21.0 %collective-permute-start.62 = (bf16[384,768]{1,0:T(8,128)(2,1)S(1)}, bf16[384,768]{1,0:T(8,128)(2,1)}, u32[]{:S(2)}, u32[]{:S(2)}) collective-permute-start(bf16[384,768]{1,0:T(8,128)(2,1)S(1)} %collective-permute-done.56.refs_6_), channel_id=1, source_target_pairs={{0,1},{1,0},{2,3},{3,2},{4,5},{5,4},{6,7},{7,6},{8,9},{9,8},{10,11... | collective-permute-start | bytes 1769480 | tf_op jit(solution)/shard_map/ppermute | solution.py:847
  275.2 22.1 %collective-permute-start.53 = (bf16[384,768]{1,0:T(8,128)(2,1)}, bf16[384,768]{1,0:T(8,128)(2,1)}, u32[]{:S(2)}, u32[]{:S(2)}) collective-permute-start(bf16[384,768]{1,0:T(8,128)(2,1)} %collective-permute-done.50.refs_1_), channel_id=1, source_target_pairs={{0,1},{1,0},{2,3},{3,2},{4,5},{5,4},{6,7},{7,6},{8,9},{9,8},{10,11... | collective-permute-start | bytes 1769480 | tf_op jit(solution)/shard_map/ppermute | solution.py:847
  275.2 22.1 %collective-permute-start.54 = (bf16[384,768]{1,0:T(8,128)(2,1)}, bf16[384,768]{1,0:T(8,128)(2,1)}, u32[]{:S(2)}, u32[]{:S(2)}) collective-permute-start(bf16[384,768]{1,0:T(8,128)(2,1)} %collective-permute-done.52.refs_2_), channel_id=1, source_target_pairs={{0,1},{1,0},{2,3},{3,2},{4,5},{5,4},{6,7},{7,6},{8,9},{9,8},{10,11... | collective-permute-start | bytes 1769480 | tf_op jit(solution)/shard_map/ppermute | solution.py:847
  (66 other events, 791.2 us)
